TPU v7x, 32 devices: a whole 2x2x4 slice. The times are simulated.
32 devices in a mesh: wide: 8 (over z, y), narrow: 4 (over x, core).
Axes of the slice: x: 2, y: 2, z: 4, core: 2. Of those that a mesh axis runs over, the one named last changes fastest.
Arguments:
- resid: bfloat16 [128, 16384], P(('wide', 'narrow')), may hold values from -6 to 6
- queries: bfloat16 [128, 16384], P(('wide', 'narrow')), may hold values from -9 to 9
- key_cache: bfloat16 [128, 192, 1024], P(('wide', 'narrow')), may hold values from -4 to 4
- value_cache: bfloat16 [128, 192, 1024], P(('wide', 'narrow')), may hold values from -6 to 6
- new_keys: bfloat16 [128, 1024], P(('wide', 'narrow')), may hold values from -4 to 4
- new_values: bfloat16 [128, 1024], P(('wide', 'narrow')), may hold values from -6 to 6
- lengths: int32 [128], P(('wide', 'narrow')), may hold values from 2 to 192, as said below
- norm_gain: bfloat16 [16384], replicated, may hold values from 0.099609375 to 1.8984375
- w_gate: bfloat16 [16384, 28672], P('narrow', 'wide'), may hold values from -0.046875 to 0.046875
- w_up: bfloat16 [16384, 28672], P('narrow', 'wide'), may hold values from -0.046875 to 0.046875
- w_down: bfloat16 [28672, 16384], P('wide', 'narrow'), may hold values from -0.03125 to 0.03125
Outputs:
- layer_out: bfloat16 [128, 16384], P(('wide', 'narrow'))
Inputs may be any that keep to these rules, and one draw needn't show every extreme that they name: Positions below lengths[b] of sequence b are live; some sequence holds all 192.
All inputs are finite; a program needn't handle non-finite values.
Results may differ from a plain program's by a relative error of at most 0.019.
Values may be sent and summed in bfloat16 or wider, within the bound.
No kernel may reach another device: no remote copies, remote signals or barrier semaphores. Data moves between devices by JAX's collectives and lax.ppermute only.
A program may use at most 192 MiB of HBM per device.

v0:
```python
import jax
import jax.numpy as jnp
from jax import lax
from jax.sharding import PartitionSpec as P

HEADS = 128
KVH = 8
HD = 128


def attend(query_rows, key_rows, value_rows, key_new, value_new, length_rows):
    count = query_rows.shape[0]
    cached = key_rows.shape[1]
    groups = HEADS // KVH
    qh = query_rows.reshape(count, KVH, groups, HD)
    kh = key_rows.reshape(count, cached, KVH, HD)
    vh = value_rows.reshape(count, cached, KVH, HD)
    kn = key_new.reshape(count, KVH, HD)
    vn = value_new.reshape(count, KVH, HD)
    score_scale = 1.0 / HD**0.5
    scores = jnp.einsum("bgqd,btgd->bgqt", qh, kh, preferred_element_type=jnp.float32) * score_scale
    own = jnp.einsum("bgqd,bgd->bgq", qh, kn, preferred_element_type=jnp.float32) * score_scale
    live = jnp.arange(cached, dtype=jnp.int32)[None, :] < length_rows[:, None]
    live = live[:, None, None, :]
    scores = jnp.where(live, scores, jnp.float32(-1e30))
    row_top = jnp.maximum(jnp.max(scores, axis=-1), own)
    cache_exp = jnp.where(live, jnp.exp(scores - row_top[..., None]), jnp.float32(0.0))
    own_exp = jnp.exp(own - row_top)
    total = jnp.sum(cache_exp, axis=-1) + own_exp
    probs = (cache_exp / total[..., None]).astype(jnp.bfloat16)
    own_prob = (own_exp / total).astype(jnp.bfloat16)
    attended = jnp.einsum("bgqt,btgd->bgqd", probs, vh, preferred_element_type=jnp.float32)
    attended = (
        attended + own_prob.astype(jnp.float32)[..., None] * vn.astype(jnp.float32)[:, :, None, :]
    )
    return attended.reshape(count, HEADS * HD)


def gated(pair_sums, hidden_width):
    return (jax.nn.silu(pair_sums[:, :hidden_width]) * pair_sums[:, hidden_width:]).astype(
        jnp.bfloat16
    )


def body(
    resid,
    queries,
    key_cache,
    value_cache,
    new_keys,
    new_values,
    lengths,
    norm_gain,
    w_gate,
    w_up,
    w_down,
):
    attended = attend(queries, key_cache, value_cache, new_keys, new_values, lengths)
    mixed = resid.astype(jnp.float32) + attended
    mean_square = jnp.mean(mixed * mixed, axis=-1, keepdims=True)
    normed = (mixed * lax.rsqrt(mean_square + 1e-05) * norm_gain.astype(jnp.float32)).astype(
        jnp.bfloat16
    )
    regrouped = lax.all_to_all(normed, "narrow", split_axis=1, concat_axis=0, tiled=True)
    piece = lax.all_gather(regrouped, "wide", axis=0, tiled=True)
    gate_part = jnp.dot(piece, w_gate, preferred_element_type=jnp.float32)
    up_part = jnp.dot(piece, w_up, preferred_element_type=jnp.float32)
    partial_value = jnp.concatenate([gate_part, up_part], axis=1)
    hidden_width = w_gate.shape[1]
    summed = lax.psum(partial_value.astype(jnp.bfloat16), "narrow").astype(jnp.float32)
    hidden = gated(summed, hidden_width)
    reduced = lax.psum_scatter(
        jnp.dot(hidden, w_down, preferred_element_type=jnp.float32).astype(jnp.bfloat16),
        "wide",
        scatter_dimension=0,
        tiled=True,
    )
    ffn_out = lax.all_to_all(reduced, "narrow", split_axis=0, concat_axis=1, tiled=True)
    return (mixed + ffn_out.astype(jnp.float32)).astype(jnp.bfloat16)


def solution(mesh):
    return jax.shard_map(
        body,
        mesh=mesh,
        in_specs=(
            P(("wide", "narrow"), None),
            P(("wide", "narrow"), None),
            P(("wide", "narrow"), None, None),
            P(("wide", "narrow"), None, None),
            P(("wide", "narrow"), None),
            P(("wide", "narrow"), None),
            P(("wide", "narrow")),
            P(),
            P("narrow", "wide"),
            P("narrow", "wide"),
            P("wide", "narrow"),
        ),
        out_specs=P(("wide", "narrow"), None),
        check_vma=False,
    )
```

profile of v0, /device:TPU:0, one launch (start us, length us, event | category | flops | bytes accessed | tf_op | source)
XLA Modules:
  0.0 232.0 jit_solution(16391475829681570030)
XLA Ops:
  6.5 0.9 iota_compare_fusion
  7.4 0.8 reshape.70
  8.2 0.7 convert_bitcast_fusion
  8.9 0.8 convert_element_type.56
  9.7 0.9 copy.23
  10.8 1.0 fusion.27
  11.8 0.3 fusion.18
  12.1 0.6 fusion.13
  12.7 0.3 copy-done.3
  13.0 0.3 multiply_reduce_fusion
  13.3 0.3 multiply_convert_fusion
  13.6 8.6 %all_to_all.32 = bf16[4,4,4096]{2,0,1:T(4,128)(2,1)S(1)} all-to-all(bf16[4,4,4096]{2,0,1:T(4,128)(2,1)S(1)} %bitcast.62), channel_id=1, replica_groups=mesh['wide'=8,'narrow'=4] {'narrow'}, dimensions={1} | all-to-all | bytes 262144 | tf_op jit(solution)/shard_map/all_to_all | solution.py:64
  22.2 0.7 all_to_all.27
  23.0 40.6 %all-gather.2.cloned.1.call-done = bf16[128,4096]{1,0:T(8,128)(2,1)} async-done(((bf16[16,4096]{1,0:T(8,128)(2,1)}), bf16[128,4096]{1,0:T(8,128)(2,1)}) %all-gather.2.cloned.1.call-update) | async-done | bytes 1048592 | tf_op jit(solution)/shard_map/all_gather | solution.py:65
  63.6 13.7 %convolution_convert_fusion.1 = bf16[128,3584]{1,0:T(8,128)(2,1)S(1)} fusion(bf16[128,4096]{1,0:T(8,128)(2,1)} %all-gather.2.cloned.1.call-done, bf16[4096,3584]{1,0:T(8,128)(2,1)} %param.20), kind=kOutput, calls=%fused_computation.1 | convolution fusion | flops 3758555136 | bytes 31326208 | tf_op jit(solution)/shard_map/dot_general | solution.py:67
  77.3 11.6 %convolution_convert_fusion.2 = bf16[128,3584]{1,0:T(8,128)(2,1)S(1)} fusion(bf16[128,4096]{1,0:T(8,128)(2,1)S(1)} %copy-done.2, bf16[4096,3584]{1,0:T(8,128)(2,1)} %param.19), kind=kOutput, calls=%fused_computation.2 | convolution fusion | flops 3758555136 | bytes 31326208 | tf_op jit(solution)/shard_map/dot_general | solution.py:66
  88.9 1.4 pad_maximum_fusion
  90.6 45.8 %all-reduce.2.cloned.1.call-done = bf16[128,7168]{1,0:T(8,128)(2,1)} async-done(((bf16[128,7168]{1,0:T(8,128)(2,1)}), bf16[128,7168]{1,0:T(8,128)(2,1)}) %all-reduce.2.cloned.1.call-update) | async-done | bytes 1835024 | tf_op jit(solution)/shard_map/psum | solution.py:70
  136.4 1.9 convert_element_type.58
  138.3 14.5 %convolution_convert_fusion = bf16[128,4096]{1,0:T(8,128)(2,1)} fusion(bf16[3584,4096]{1,0:T(8,128)(2,1)} %param.21, f32[128,7168]{1,0:T(8,128)S(1)} %convert_element_type.58), kind=kOutput, calls=%fused_computation | convolution fusion | flops 3761373184 | bytes 34078720 | tf_op jit(solution)/shard_map/dot_general | solution.py:73
  152.8 63.6 %reduce-scatter.2.cloned.1.call-done = bf16[16,4096]{1,0:T(8,128)(2,1)} async-done(((bf16[128,4096]{1,0:T(8,128)(2,1)}), bf16[16,4096]{1,0:T(8,128)(2,1)}) %reduce-scatter.2.cloned.1.call-update) | async-done | bytes 131088 | tf_op jit(solution)/shard_map/reduce_scatter | solution.py:72
  216.4 1.0 all_to_all.28
  217.3 7.2 %all_to_all.33 = bf16[4,4,4096]{2,1,0:T(4,128)(2,1)S(1)} all-to-all(bf16[4,4,4096]{2,1,0:T(4,128)(2,1)S(1)} %all_to_all.28), channel_id=1, replica_groups=mesh['wide'=8,'narrow'=4] {'narrow'}, dimensions={0} | all-to-all | bytes 262144 | tf_op jit(solution)/shard_map/all_to_all | solution.py:78
  224.5 0.9 add_convert_fusion
  (21 shorter events, 0.6 us)
Async XLA Ops:
  6.5 4.2 %copy-start = (bf16[4,192,1024]{2,1,0:T(8,128)(2,1)S(1)}, bf16[4,192,1024]{2,1,0:T(8,128)(2,1)}, u32[]{:S(2)}) copy-start(bf16[4,192,1024]{2,1,0:T(8,128)(2,1)} %param.13) | copy-start | bytes 4718596
  6.5 5.6 %copy-start.4 = (bf16[4,192,1024]{2,1,0:T(8,128)(2,1)S(1)}, bf16[4,192,1024]{2,1,0:T(8,128)(2,1)}, u32[]{:S(2)}) copy-start(bf16[4,192,1024]{2,1,0:T(8,128)(2,1)} %param.14) | copy-start | bytes 4718596
  6.5 57.0 %all-gather.2.cloned.1.call-start = ((), (), s32[]{:S(2)}) async-start(), calls=%async_computation.3 | async-start | bytes 1179648 | tf_op jit(solution)/shard_map/all_gather | solution.py:65
  12.1 0.9 copy-start.3
  22.9 113.4 %all-reduce.2.cloned.1.call-start = ((), (), s32[]{:S(2)}) async-start(), calls=%async_computation.4 | async-start | bytes 3670016 | tf_op jit(solution)/shard_map/psum | solution.py:70
  63.6 13.7 %copy-start.2 = (bf16[128,4096]{1,0:T(8,128)(2,1)S(1)}, bf16[128,4096]{1,0:T(8,128)(2,1)}, u32[]{:S(2)}) copy-start(bf16[128,4096]{1,0:T(8,128)(2,1)} %all-gather.2.cloned.1.call-done) | copy-start | bytes 3145732
  90.3 126.0 %reduce-scatter.2.cloned.1.call-start = ((), (), s32[]{:S(2)}) async-start(), calls=%async_computation.5 | async-start | bytes 1179648 | tf_op jit(solution)/shard_map/reduce_scatter | solution.py:72
  138.2 87.2 %copy-start.1 = (bf16[4,192,1024]{2,1,0:T(8,128)(2,1)S(1)}, bf16[4,192,1024]{2,1,0:T(8,128)(2,1)}, u32[]{:S(2)}) copy-start(bf16[4,192,1024]{2,1,0:T(8,128)(2,1)} %param.13) | copy-start | bytes 4718596
Sparse Core Ops, SparseCore 0:
  23.1 40.4 all-gather.1
  90.5 45.8 all-reduce.1
  152.9 63.4 reduce-scatter.1
where the time goes:
time: 232 us
  waiting for transfers between devices  150 us (65%)
  matrix products  41.6 us (18%)
  blocking collectives  15.8 us (7%)
  between operations  13.2 us (6%)
  other arithmetic  7.37 us (3%)
  local copies, waits for them, and re-layouts  3.68 us (2%)
    reduce_scatter x1, waiting for transfers between devices, body(): lax.psum_scatter(jnp.dot(hidden, w_down, preferred_element_type=jnp.float...  63.6 us
    psum x1, waiting for transfers between devices, body(): lax.psum(partial_value.astype(jnp.bfloat16), 'narrow').astype(jnp.float32)  45.8 us
    all_gather x1, waiting for transfers between devices, body(): piece = lax.all_gather(regrouped, 'wide', axis=0, tiled=True)  40.6 us
    dot_general x1, matrix products, body(): jnp.dot(hidden, w_down, preferred_element_type=jnp.float32)  14.5 us
    dot_general x1, matrix products, body(): up_part = jnp.dot(piece, w_up, preferred_element_type=jnp.float32)  13.7 us
    dot_general x1, matrix products, body(): gate_part = jnp.dot(piece, w_gate, preferred_element_type=jnp.float32)  11.6 us
    all_to_all x1, blocking collectives, body(): lax.all_to_all(normed, 'narrow', split_axis=1, concat_axis=0, tiled=True)  8.64 us
    all_to_all x1, blocking collectives, body(): lax.all_to_all(reduced, 'narrow', split_axis=0, concat_axis=1, tiled=True)  7.16 us
  transfers between devices with their start and end apart: 3, of which 3 were waited for; matrix products, arithmetic and copies ran while one was open for 0% of the time, Pallas kernels for 0%

commit v1 on v0

v1 whole, which is shorter than its diff:
```python
import jax
import jax.numpy as jnp
from jax import lax
from jax.experimental import pallas as pl
from jax.experimental.pallas import tpu as pltpu
from jax.sharding import PartitionSpec as P

HEADS = 128
KVH = 8
HD = 128
F32 = jnp.float32
BF16 = jnp.bfloat16
COST = 16
SCOPED = 3 << 20
def tile_of(width):
    for tile in (512, 256, 128):
        if width % tile == 0:
            return tile
    return width


def after(x, *others):
    return lax.optimization_barrier((x, *others))[0]


SCALAR = pl.BlockSpec(memory_space=pltpu.SMEM)
FAST = pl.BlockSpec(memory_space=pltpu.VMEM)
SLOW = pl.BlockSpec(memory_space=pltpu.HBM)
ANY = pl.BlockSpec(memory_space=pl.ANY)


class Piece:
    def __init__(self, weight, row, rows, column, columns):
        self.weight = weight
        self.row, self.rows, self.column, self.columns = row, rows, column, columns


def call(kernel, name, flags, inputs, outputs, ahead, scratch, flops, behind):
    weights = []
    for piece in ahead:
        if not any(piece.weight is w for w in weights):
            weights.append(piece.weight)
    source = [next(i for i, w in enumerate(weights) if w is p.weight) for p in ahead]
    n_in, n_w, n_out, n_a = len(inputs), len(weights), len(outputs), len(ahead)

    def whole(*refs):
        flag_ref, refs = refs[0], refs[1:]
        in_refs, refs = refs[:n_in], refs[n_in + len(behind) :]
        weight_refs, refs = refs[:n_w], refs[n_w:]
        out_refs, refs = refs[:n_out], refs[n_out:]
        ahead_refs, refs = refs[:n_a], refs[n_a:]
        sems, scratch_refs = refs[0], refs[1:]
        copies = []
        for i, piece in enumerate(ahead):
            view = weight_refs[source[i]].at[
                pl.ds(piece.row, piece.rows), pl.ds(piece.column, piece.columns)
            ]
            copies.append(pltpu.make_async_copy(view, ahead_refs[i], sems.at[i]))
        for copy in copies:
            copy.start()
        kernel(flag_ref, in_refs, out_refs, scratch_refs)
        for copy in copies:
            copy.wait()

    moved = sum(2 * p.rows * p.columns for p in ahead)
    result = pl.pallas_call(
        whole,
        in_specs=[SCALAR, *[FAST] * n_in, *[ANY] * len(behind), *[SLOW] * n_w],
        out_specs=[FAST] * (n_out + n_a),
        out_shape=[*outputs, *[jax.ShapeDtypeStruct((p.rows, p.columns), BF16) for p in ahead]],
        scratch_shapes=[pltpu.SemaphoreType.DMA((max(1, n_a),)), *scratch],
        compiler_params=pltpu.CompilerParams(vmem_limit_bytes=SCOPED),
        cost_estimate=pl.CostEstimate(
            flops=flops // COST, bytes_accessed=moved // COST, transcendentals=0
        ),
        name=name,
    )(flags, *inputs, *behind, *[pltpu.with_memory_space_constraint(w, pltpu.HBM) for w in weights])
    return result[:n_out], result[n_out:]


def load(flags, ahead, behind):
    def kernel(flag_ref, in_refs, out_refs, scratch_refs):
        out_refs[0][...] = jnp.full((8, 128), flag_ref[0], jnp.int32)

    (done,), pieces = call(
        kernel,
        "load",
        flags,
        [],
        [jax.ShapeDtypeStruct((8, 128), jnp.int32)],
        ahead,
        [],
        0,
        behind,
    )
    return done, pieces


def attend(lengths, queries, keys, values, new_keys, new_values, resid):
    count, width = queries.shape
    cached = keys.shape[1]
    heads = width // HD
    groups = heads // KVH
    score_scale = 1.0 / HD**0.5
    inputs = (lengths, queries, keys, new_keys, values, new_values, resid)

    def kernel(*refs):
        slow_refs, refs = refs[: len(inputs)], refs[len(inputs) :]
        mixed_ref, square_ref, *fast_refs, sems = refs
        length_ref, q_ref, k_ref, kn_ref, v_ref, vn_ref, resid_ref = fast_refs
        copies = [
            pltpu.make_async_copy(slow, fast, sems.at[i])
            for i, (slow, fast) in enumerate(zip(slow_refs, fast_refs, strict=True))
        ]
        for copy in copies:
            copy.start()
        position = lax.broadcasted_iota(jnp.int32, (heads, cached), 1)

        def rows_of(ref, b):
            row = ref[b : b + 1, :].astype(F32)
            return jnp.concatenate(
                [
                    jnp.broadcast_to(row[:, g * HD : (g + 1) * HD], (groups, HD))
                    for g in range(KVH)
                ],
                axis=0,
            )

        for copy in copies[:4]:
            copy.wait()
        weights = []
        for b in range(count):
            q = q_ref[b : b + 1, :].astype(F32).reshape(heads, HD)
            q_narrow = q.astype(BF16)
            scores = [
                lax.dot_general(
                    q_narrow[g * groups : (g + 1) * groups],
                    k_ref[b, :, g * HD : (g + 1) * HD],
                    (((1,), (1,)), ((), ())),
                    preferred_element_type=F32,
                )
                for g in range(KVH)
            ]
            scores = jnp.concatenate(scores, axis=0) * score_scale
            own = jnp.sum(q * rows_of(kn_ref, b), axis=-1, keepdims=True) * score_scale
            live = position < length_ref[b]
            scores = jnp.where(live, scores, jnp.float32(-1e30))
            top = jnp.maximum(jnp.max(scores, axis=-1, keepdims=True), own)
            cache_exp = jnp.where(live, jnp.exp(scores - top), jnp.float32(0.0))
            own_exp = jnp.exp(own - top)
            total = jnp.sum(cache_exp, axis=-1, keepdims=True) + own_exp
            weights.append(
                ((cache_exp / total).astype(BF16), (own_exp / total).astype(BF16).astype(F32))
            )
        for copy in copies[4:]:
            copy.wait()
        for b in range(count):
            probs, own_prob = weights[b]
            attended = [
                jnp.dot(
                    probs[g * groups : (g + 1) * groups],
                    v_ref[b, :, g * HD : (g + 1) * HD],
                    preferred_element_type=F32,
                )
                for g in range(KVH)
            ]
            mixed = jnp.concatenate(attended, axis=0) + own_prob * rows_of(vn_ref, b)
            mixed = mixed + resid_ref[b : b + 1, :].astype(F32).reshape(heads, HD)
            mean_square = jnp.sum(mixed * mixed, keepdims=True) * (1.0 / width)
            mixed_ref[b : b + 1, :] = mixed.reshape(1, width)
            square_ref[b : b + 1, :] = jnp.broadcast_to(mean_square, (1, HD))

    fast = [pltpu.VMEM(x.shape, x.dtype) for x in inputs]
    fast[0] = pltpu.SMEM(lengths.shape, lengths.dtype)
    return pl.pallas_call(
        kernel,
        in_specs=[SLOW] * len(inputs),
        out_specs=[FAST, FAST],
        out_shape=[
            jax.ShapeDtypeStruct((count, width), F32),
            jax.ShapeDtypeStruct((count, HD), F32),
        ],
        scratch_shapes=[*fast, pltpu.SemaphoreType.DMA((len(inputs),))],
        compiler_params=pltpu.CompilerParams(vmem_limit_bytes=16 << 20),
        name="attend",
    )(*[pltpu.with_memory_space_constraint(x, pltpu.HBM) for x in inputs])


def gate_up(core, x, gates, ups, ahead, behind):
    rows, depth = x.shape
    half = rows // 2
    n, tile = len(gates), gates[0].shape[1]

    def kernel(core_ref, in_refs, out_refs, scratch_refs):
        x_ref, w_refs = in_refs[0], (in_refs[1 : n + 1], in_refs[n + 1 :])
        keep_ref, send_ref = out_refs
        upper = core_ref[0] == 0
        for j in range(n):
            at = slice(j * tile, (j + 1) * tile)
            for i in range(2):
                part = jnp.dot(x_ref[...], w_refs[i][j][...], preferred_element_type=F32)
                keep_ref[i, :, at] = jnp.where(upper, part[:half], part[half:])
                send_ref[i, :, at] = jnp.where(upper, part[half:], part[:half]).astype(BF16)

    return call(
        kernel,
        "gate_up",
        core,
        [x, *gates, *ups],
        [
            jax.ShapeDtypeStruct((2, half, n * tile), F32),
            jax.ShapeDtypeStruct((2, half, n * tile), BF16),
        ],
        ahead,
        [],
        4 * rows * depth * n * tile,
        behind,
    )


def down(core, mine, theirs, sums, weights, first, count, tile, split, ahead, behind):
    half = mine[0].shape[0]
    widths = [t.shape[1] for t in mine]
    n = len(mine)
    shapes = jax.eval_shape(split, jax.ShapeDtypeStruct((2 * half, tile), F32))
    with_sums = [] if sums is None else [sums]

    def kernel(core_ref, in_refs, out_refs, scratch_refs):
        (h_ref,) = scratch_refs
        own = pl.multiple_of(core_ref[0] * half, half)
        other = pl.multiple_of(half - core_ref[0] * half, half)
        at = 0
        for i in range(n):
            h_ref[pl.ds(own, half), at : at + widths[i]] = in_refs[i][...]
            h_ref[pl.ds(other, half), at : at + widths[i]] = in_refs[n + i][...]
            at += widths[i]
        for j in range(count):
            columns = slice((first + j) * tile, (first + j + 1) * tile)
            value, at = None, 0
            for i in range(n):
                term = jnp.dot(
                    h_ref[:, at : at + widths[i]],
                    in_refs[2 * n + i][:, columns],
                    preferred_element_type=F32,
                )
                value = term if value is None else value + term
                at += widths[i]
            for ref in in_refs[3 * n :]:
                value = value + ref[:, columns]
            for ref, part in zip(out_refs, split(value), strict=True):
                ref[:, j * tile : (j + 1) * tile] = part

    return call(
        kernel,
        "down",
        core,
        [*mine, *theirs, *weights, *with_sums],
        [jax.ShapeDtypeStruct((s.shape[0], count * tile), s.dtype) for s in shapes],
        ahead,
        [pltpu.VMEM((2 * half, sum(widths)), BF16)],
        4 * half * sum(widths) * count * tile,
        behind,
    )


def solution(mesh):
    n_wide, n_narrow = mesh.shape["wide"], mesh.shape["narrow"]
    n_far = n_wide // 2
    near_far = n_far // 2

    def narrow_swap(x, mask):
        return lax.ppermute(x, "narrow", [(i, i ^ mask) for i in range(n_narrow)])

    def wide_swap(x):
        return lax.ppermute(x, "wide", [(i, i ^ 1) for i in range(n_wide)])

    def far_swap(x, slot):
        return lax.ppermute(x, "wide", [(i, i ^ (slot << 1)) for i in range(n_wide)])

    def by_position(first, second):
        order = []
        for top in range(2):
            for side in (first, second):
                order += side[top * near_far : (top + 1) * near_far]
        return jnp.concatenate(order, axis=0)

    def from_narrow(pieces, am, j):
        out = pieces[j]
        for i in range(1, n_narrow):
            out = jnp.where(am[i], pieces[j ^ i], out)
        return out

    def body(
        resid,
        queries,
        key_cache,
        value_cache,
        new_keys,
        new_values,
        lengths,
        norm_gain,
        w_gate,
        w_up,
        w_down,
    ):
        own_rows = resid.shape[0]
        block = w_gate.shape[0]
        me = lax.axis_index("narrow").astype(jnp.uint32)
        partner = [me ^ jnp.uint32(s) for s in range(n_narrow)]
        place = (
            [p * jnp.uint32(block) for p in partner],
            [p * jnp.uint32(own_rows) for p in partner],
            [me == jnp.uint32(i) for i in range(n_narrow)],
            (me & jnp.uint32(1)).astype(jnp.int32).reshape(1),
        )
        place, queries = lax.optimization_barrier((place, queries))
        column_at, row_at, am, core = place
        tile = tile_of(w_gate.shape[1])
        tiles = w_gate.shape[1] // tile
        chunks = [[0], *[list(range(i, min(i + 2, tiles))) for i in range(1, tiles, 2)]]
        gates, ups, downs = {}, {}, {}

        def gate_up_pieces(which):
            return [
                Piece(w, 0, w.shape[0], j * tile, tile) for j in which for w in (w_gate, w_up)
            ]

        def take(which, pieces):
            for i, j in enumerate(which):
                gates[j], ups[j] = pieces[2 * i], pieces[2 * i + 1]

        def bring(which, behind):
            done, pieces = load(core, gate_up_pieces(which), behind)
            take(which, pieces)
            return done

        def down_pieces(which):
            return [
                Piece(w_down, chunks[c][0] * tile, len(chunks[c]) * tile, 0, w_down.shape[1])
                for c in which
            ]

        mixed, mean_square = attend(
            lengths, queries, key_cache, value_cache, new_keys, new_values, resid
        )
        normed = (
            mixed * lax.rsqrt(mean_square[:, :1] + 1e-05) * norm_gain.astype(F32)
        ).astype(BF16)
        def column_block(x, s):
            return lax.dynamic_slice(x, (jnp.uint32(0), column_at[s]), (own_rows, block))

        pieces = [column_block(normed, 0)]
        for s in range(1, n_narrow):
            pieces.append(narrow_swap(column_block(normed, s), s))
        group = jnp.concatenate([from_narrow(pieces, am, j) for j in range(n_narrow)], axis=0)
        group_rows = own_rows * n_narrow

        unit = tile_of(block)
        cut = (block // unit * 3 // 8) * unit
        left, right = group[:, :cut], group[:, cut:]
        pair = jnp.concatenate([left, wide_swap(left)], axis=0)
        far_right = [right] + [far_swap(right, s) for s in range(1, n_far)]
        first_done = bring([0, 1], [pair])
        pair = after(pair, far_right)
        far_pairs = [pair] + [far_swap(pair, s) for s in range(1, n_far)]
        other = wide_swap(jnp.concatenate(far_right, axis=0))
        second_done = bring([2, 3], [pair])
        far_pairs, other, second_done = lax.optimization_barrier((far_pairs, other, second_done))
        x_left = by_position(
            [p[:group_rows] for p in far_pairs], [p[group_rows:] for p in far_pairs]
        )
        x_right = by_position(
            far_right,
            [other[s * group_rows : (s + 1) * group_rows] for s in range(n_far)],
        )
        x = jnp.concatenate([x_left, x_right], axis=1)

        plan = [
            [],
            gate_up_pieces(chunks[2][1:]),
            gate_up_pieces(chunks[3]),
            down_pieces([0, 1]),
        ]
        chips, arrived, mine, theirs = [], [], [], []

        def finish(c):
            total = chips[c]
            for part in arrived[c]:
                total = total + part.astype(F32)
            hidden = (jax.nn.silu(total[0]) * total[1]).astype(BF16)
            mine.append(hidden)
            theirs.append(narrow_swap(hidden, 1))

        for c, which in enumerate(chunks):
            behind = [sent] if c else [first_done, second_done]
            (keep, send), pieces = gate_up(
                core, x, [gates[j] for j in which], [ups[j] for j in which], plan[c], behind
            )
            if c == 1:
                take(chunks[2][1:], pieces)
            elif c == 2:
                take(chunks[3], pieces)
            elif c == 3:
                downs[0], downs[1] = pieces
            if c:
                send, arrived[-1] = lax.optimization_barrier((send, arrived[-1]))
                finish(c - 1)
            chip = keep + narrow_swap(send, 1).astype(F32)
            sent = chip.astype(BF16)
            if c == len(chunks) - 1:
                sent, theirs[:2] = lax.optimization_barrier((sent, theirs[:2]))
            chips.append(chip)
            arrived.append([narrow_swap(sent, s) for s in range(2, n_narrow, 2)])

        column_tile = tile_of(w_down.shape[1])
        column_tiles = w_down.shape[1] // column_tile
        sums = None
        for low, high in ((0, 2), (2, 3)):
            (sums,), pieces = down(
                core,
                mine[low:high],
                theirs[low:high],
                sums,
                [downs[i] for i in range(low, high)],
                0,
                column_tiles,
                column_tile,
                lambda value: (value,),
                down_pieces([2, 3]) if low == 0 else [],
                [],
            )
            if low == 0:
                downs[2], downs[3] = pieces
        sums, arrived[-1] = lax.optimization_barrier((sums, arrived[-1]))
        finish(len(chunks) - 1)

        near_tiles = column_tiles * 5 // 8
        run = near_far * group_rows

        def split_near(value):
            kept = [value[2 * top * run : (2 * top + 1) * run] for top in range(2)]
            sent = [value[(2 * top + 1) * run : (2 * top + 2) * run] for top in range(2)]
            return jnp.concatenate(kept, axis=0), jnp.concatenate(sent, axis=0).astype(BF16)

        def split_far(value):
            out = []
            for top in range(2):
                for low in range(near_far):
                    at = 2 * top * run + low * group_rows
                    both = [value[i : i + group_rows] for i in (at, at + run)]
                    out.append(jnp.concatenate(both, axis=0))
            return (out[0], *[part.astype(BF16) for part in out[1:]])

        (kept, sent), _ = down(
            core,
            mine[3:],
            theirs[3:],
            sums,
            [downs[3]],
            0,
            near_tiles,
            column_tile,
            split_near,
            [],
            [],
        )
        far_parts, _ = down(
            core,
            mine[3:],
            theirs[3:],
            sums,
            [downs[3]],
            near_tiles,
            column_tiles - near_tiles,
            column_tile,
            split_far,
            [],
            [sent],
        )
        near_sum = kept + wide_swap(sent).astype(F32)
        near_sent = near_sum.astype(BF16)
        left_sum = near_sum[:group_rows]
        right_parts = [far_swap(far_parts[s], s) for s in range(1, n_far)]
        left_parts = [
            far_swap(near_sent[s * group_rows : (s + 1) * group_rows], s) for s in range(1, n_far)
        ]
        right_parts, left_parts[0] = lax.optimization_barrier((right_parts, left_parts[0]))
        right_sum = far_parts[0]
        for part in right_parts:
            right_sum = right_sum + part.astype(F32)
        for part in left_parts:
            left_sum = left_sum + part.astype(F32)
        right_sum = right_sum[:group_rows] + wide_swap(
            right_sum[group_rows:].astype(BF16)
        ).astype(F32)
        reduced = jnp.concatenate([left_sum, right_sum], axis=1).astype(BF16)

        def row_block(x, s):
            return lax.dynamic_slice(x, (row_at[s], jnp.uint32(0)), (own_rows, block))

        pieces = [row_block(reduced, 0)]
        for s in range(1, n_narrow):
            pieces.append(narrow_swap(row_block(reduced, s), s))
        ffn_out = jnp.concatenate([from_narrow(pieces, am, j) for j in range(n_narrow)], axis=1)
        return (mixed + ffn_out.astype(F32)).astype(BF16)

    return jax.shard_map(
        body,
        mesh=mesh,
        in_specs=(
            P(("wide", "narrow"), None),
            P(("wide", "narrow"), None),
            P(("wide", "narrow"), None, None),
            P(("wide", "narrow"), None, None),
            P(("wide", "narrow"), None),
            P(("wide", "narrow"), None),
            P(("wide", "narrow")),
            P(),
            P("narrow", "wide"),
            P("narrow", "wide"),
            P("wide", "narrow"),
        ),
        out_specs=P(("wide", "narrow"), None),
        check_vma=False,
    )
```

time: 232 us -> 106 us (0.46)
  waiting for transfers between devices: 150 us -> 25.9 us
  Pallas kernels: 0 us -> 42.9 us
  matrix products: 41.6 us -> 0 us
  starting transfers between devices: 0.27 us -> 32.6 us
  blocking collectives: 15.8 us -> 0 us
  between operations: 13.2 us -> 0.52 us
  other arithmetic: 7.37 us -> 3.76 us
  local copies, waits for them, and re-layouts: 3.68 us -> 0.25 us
    reduce_scatter x1 -> x0, waiting for transfers between devices: 63.6 us -> none  [body(): lax.psum_scatter(jnp.dot(hidden, w_down, preferred_element_type=jnp.float...]
    psum x1 -> x0, waiting for transfers between devices: 45.8 us -> none  [body(): lax.psum(partial_value.astype(jnp.bfloat16), 'narrow').astype(jnp.float32)]
    pallas_call x0 -> x11, Pallas kernels: none -> 42.9 us  [the longest x10 39.6 us: call(): pl.pallas_call(whole, in_specs=[SCALAR, *[FAST] * n_in, *[ANY] * len(behi...]
    dot_general x6 -> x0, matrix products: 41.6 us -> none  [the longest x1 14.5 us: body(): jnp.dot(hidden, w_down, preferred_element_type=jnp.float32)]
    all_gather x1 -> x0, waiting for transfers between devices: 40.6 us -> none  [body(): piece = lax.all_gather(regrouped, 'wide', axis=0, tiled=True)]
    ppermute x0 -> x34, starting transfers between devices: none -> 32.6 us  [the longest x12 17.4 us: far_swap(): return lax.ppermute(x, 'wide', [(i, i ^ slot << 1) for i in range(n_wide)])]
    ppermute x0 -> x34, waiting for transfers between devices: none -> 25.9 us  [the longest x18 14.5 us: narrow_swap(): return lax.ppermute(x, 'narrow', [(i, i ^ mask) for i in range(n_narrow)])]
    all_to_all x2 -> x0, blocking collectives: 15.8 us -> none  [the longest x1 8.64 us: body(): lax.all_to_all(normed, 'narrow', split_axis=1, concat_axis=0, tiled=True)]
  transfers between devices with their start and end apart: 3 -> 34, of which waited for: 3 -> 16; matrix products, arithmetic and copies ran while one was open for 0% -> 1% of each run, Pallas kernels for 0% -> 35%
where the time goes in v1:
time: 106 us
  Pallas kernels  42.9 us (40%)
  starting transfers between devices  32.6 us (31%)
  waiting for transfers between devices  25.9 us (24%)
  other arithmetic  3.76 us (4%)
    pallas_call x10, Pallas kernels, call(): pl.pallas_call(whole, in_specs=[SCALAR, *[FAST] * n_in, *[ANY] * len(behi...  39.6 us
    ppermute x12, starting transfers between devices, far_swap(): return lax.ppermute(x, 'wide', [(i, i ^ slot << 1) for i in range(n_wide)])  17.4 us
    ppermute x18, waiting for transfers between devices, narrow_swap(): return lax.ppermute(x, 'narrow', [(i, i ^ mask) for i in range(n_narrow)])  14.5 us
    ppermute x18, starting transfers between devices, narrow_swap(): return lax.ppermute(x, 'narrow', [(i, i ^ mask) for i in range(n_narrow)])  11.1 us
    ppermute x12, waiting for transfers between devices, far_swap(): return lax.ppermute(x, 'wide', [(i, i ^ slot << 1) for i in range(n_wide)])  6.46 us
    ppermute x4, waiting for transfers between devices, wide_swap(): return lax.ppermute(x, 'wide', [(i, i ^ 1) for i in range(n_wide)])  4.91 us
    ppermute x4, starting transfers between devices, wide_swap(): return lax.ppermute(x, 'wide', [(i, i ^ 1) for i in range(n_wide)])  4.12 us
    pallas_call x1, Pallas kernels, attend(): pl.pallas_call(kernel, in_specs=[SLOW] * len(inputs), out_specs=[FAST, FA...  3.32 us
  transfers between devices with their start and end apart: 34, of which 16 were waited for; matrix products, arithmetic and copies ran while one was open for 1% of the time, Pallas kernels for 35%

profile of v1, /device:TPU:0, one launch (start us, length us, event | category | flops | bytes accessed | tf_op | source)
XLA Modules:
  0.0 105.8 jit_solution(11136141701101540599)
XLA Ops:
  0.8 3.3 %attend.1 = (f32[4,16384]{1,0:T(4,128)S(1)}, f32[4,128]{1,0:T(4,128)S(1)}) custom-call(s32[4]{0:T(128)} %refs_0_.1, bf16[4,16384]{1,0:T(4,128)(2,1)} %refs_1_, bf16[4,192,1024]{2,1,0:T(8,128)(2,1)} %refs_2_.3, bf16[4,1024]{1,0:T(4,128)(2,1)} %refs_3_.3, bf16[4,192,1024]{2,1,0:T(8,128)(2,1)} %refs_4_.1, bf16[4,1024]{1,0:T(4,128)(2,1)} %refs_5_.1, ...), custom_call_target="tpu_custom_call" | custom-call | tf_op jit(solution)/shard_map/attend/pallas_call | solution.py:175
  4.5 2.4 %collective-permute-start = (bf16[4,4096]{1,0:T(4,128)(2,1)S(1)}, bf16[4,4096]{1,0:T(4,128)(2,1)S(1)}, u32[]{:S(2)}, u32[]{:S(2)}) collective-permute-start(bf16[4,4096]{1,0:T(4,128)(2,1)S(1)} %get-tuple-element.168), channel_id=1, source_target_pairs={{0,3},{1,2},{2,1},{3,0},{4,7},{5,6},{6,5},{7,4},{8,11},{9,10},{10,... | collective-permute-start | bytes 98312 | tf_op jit(solution)/shard_map/ppermute | solution.py:272
  8.7 2.8 %collective-permute-done.1 = bf16[4,4096]{1,0:T(4,128)(2,1)S(1)} collective-permute-done((bf16[4,4096]{1,0:T(4,128)(2,1)S(1)}, bf16[4,4096]{1,0:T(4,128)(2,1)S(1)}, u32[]{:S(2)}, u32[]{:S(2)}) %collective-permute-start.1) | collective-permute-done | bytes 32800 | tf_op jit(solution)/shard_map/ppermute | solution.py:272
  11.7 1.6 %collective-permute-start.3 = (bf16[16,1536]{1,0:T(8,128)(2,1)S(1)}, bf16[16,1536]{1,0:T(8,128)(2,1)S(1)}, u32[]{:S(2)}, u32[]{:S(2)}) collective-permute-start(bf16[16,1536]{1,0:T(8,128)(2,1)S(1)} %pad_maximum_fusion.6), channel_id=1, source_target_pairs={{0,4},{4,0},{8,12},{12,8},{16,20},{20,16},{24,28},{28,24},{1,5},{5... | collective-permute-start | bytes 147464 | tf_op jit(solution)/shard_map/ppermute | solution.py:275
  13.3 3.7 %collective-permute-start.6 = (bf16[16,2560]{1,0:T(8,128)(2,1)S(1)}, bf16[16,2560]{1,0:T(8,128)(2,1)S(1)}, u32[]{:S(2)}, u32[]{:S(2)}) collective-permute-start(bf16[16,2560]{1,0:T(8,128)(2,1)S(1)} %get-tuple-element.154), channel_id=1, source_target_pairs={{0,24},{4,28},{8,16},{12,20},{16,8},{20,12},{24,0},{28,4},{1,25},{... | collective-permute-start | bytes 245768 | tf_op jit(solution)/shard_map/ppermute | solution.py:278
  17.8 5.9 %load.3 = (s32[8,128]{1,0:T(8,128)S(1)}, bf16[4096,512]{1,0:T(8,128)(2,1)S(1)}, bf16[4096,512]{1,0:T(8,128)(2,1)S(1)}, bf16[4096,512]{1,0:T(8,128)(2,1)S(1)}, bf16[4096,512]{1,0:T(8,128)(2,1)S(1)}) custom-call(s32[1]{0:T(128)} %bitcast.refs_0_, bf16[32,1536]{1,0:T(8,128)(2,1)S(1)} %pad_maximum_fusion.2.refs_1_, bf16[4096,3584]{1,0:T(8,128)(2,1)} %refs_7_.5, ...), custom_call_target="tpu_custom_call" | custom-call | bytes 1048576 | tf_op jit(solution)/shard_map/load/pallas_call | solution.py:66
  23.8 3.7 %collective-permute-start.9 = (bf16[32,1536]{1,0:T(8,128)(2,1)S(1)}, bf16[32,1536]{1,0:T(8,128)(2,1)S(1)}, u32[]{:S(2)}, u32[]{:S(2)}) collective-permute-start(bf16[32,1536]{1,0:T(8,128)(2,1)S(1)} %pad_maximum_fusion.2.refs_1_), channel_id=1, source_target_pairs={{0,24},{4,28},{8,16},{12,20},{16,8},{20,12},{24,0},{28,4},{1,25},{... | collective-permute-start | bytes 294920 | tf_op jit(solution)/shard_map/ppermute | solution.py:278
  28.9 6.0 %load.2 = (s32[8,128]{1,0:T(8,128)S(1)}, bf16[4096,512]{1,0:T(8,128)(2,1)S(1)}, bf16[4096,512]{1,0:T(8,128)(2,1)S(1)}, bf16[4096,512]{1,0:T(8,128)(2,1)S(1)}, bf16[4096,512]{1,0:T(8,128)(2,1)S(1)}) custom-call(s32[1]{0:T(128)} %bitcast.refs_0_, bf16[32,1536]{1,0:T(8,128)(2,1)S(1)} %pad_maximum_fusion.2.refs_1_, bf16[4096,3584]{1,0:T(8,128)(2,1)} %refs_7_.5, ...), custom_call_target="tpu_custom_call" | custom-call | bytes 1048576 | tf_op jit(solution)/shard_map/load/pallas_call | solution.py:66
  35.9 1.3 %gate_up.4 = (f32[2,64,512]{2,1,0:T(8,128)S(1)}, bf16[2,64,512]{2,1,0:T(8,128)(2,1)S(1)}) custom-call(s32[1]{0:T(128)} %bitcast.refs_0_, bf16[128,4096]{1,0:T(8,128)(2,1)S(1)} %pad_maximum_fusion.refs_1_, bf16[4096,512]{1,0:T(8,128)(2,1)S(1)} %get-tuple-element.100.refs_2_, bf16[4096,512]{1,0:T(8,128)(2,1)S(1)} %get-tuple-element.101.refs_3_, ...), custom_call_target="tpu_custom_call" | custom-call | flops 67108864 | tf_op jit(solution)/shard_map/gate_up/pallas_call | solution.py:66
  37.3 1.3 %collective-permute-done.11 = bf16[2,64,512]{2,1,0:T(8,128)(2,1)S(1)} collective-permute-done((bf16[2,64,512]{2,1,0:T(8,128)(2,1)S(1)}, bf16[2,64,512]{2,1,0:T(8,128)(2,1)S(1)}, u32[]{:S(2)}, u32[]{:S(2)}) %collective-permute-start.11) | collective-permute-done | bytes 131104 | tf_op jit(solution)/shard_map/ppermute | solution.py:272
  39.7 3.5 %gate_up.5 = (f32[2,64,1024]{2,1,0:T(8,128)S(1)}, bf16[2,64,1024]{2,1,0:T(8,128)(2,1)S(1)}, bf16[4096,512]{1,0:T(8,128)(2,1)S(1)}, bf16[4096,512]{1,0:T(8,128)(2,1)S(1)}) custom-call(s32[1]{0:T(128)} %bitcast.refs_0_, bf16[128,4096]{1,0:T(8,128)(2,1)S(1)} %pad_maximum_fusion.refs_1_, bf16[4096,512]{1,0:T(8,128)(2,1)S(1)} %get-tuple-element.96.refs_2_, ...), custom_call_target="tpu_custom_call" | custom-call | flops 134217728 | bytes 524288 | tf_op jit(solution)/shard_map/gate_up/pallas_call | solution.py:66
  44.3 1.5 %collective-permute-done.13 = bf16[2,64,1024]{2,1,0:T(8,128)(2,1)S(1)} collective-permute-done((bf16[2,64,1024]{2,1,0:T(8,128)(2,1)S(1)}, bf16[2,64,1024]{2,1,0:T(8,128)(2,1)S(1)}, u32[]{:S(2)}, u32[]{:S(2)}) %collective-permute-start.13) | collective-permute-done | bytes 262176 | tf_op jit(solution)/shard_map/ppermute | solution.py:272
  46.9 8.1 %gate_up.6 = (f32[2,64,1024]{2,1,0:T(8,128)S(1)}, bf16[2,64,1024]{2,1,0:T(8,128)(2,1)S(1)}, bf16[4096,512]{1,0:T(8,128)(2,1)S(1)}, bf16[4096,512]{1,0:T(8,128)(2...) custom-call(s32[1]{0:T(128)} %bitcast.refs_0_, bf16[128,4096]{1,0:T(8,128)(2,1)S(1)} %pad_maximum_fusion.refs_1_, ...), custom_call_target="tpu_custom_call" | custom-call | flops 134217728 | bytes 1048576 | tf_op jit(solution)/shard_map/gate_up/pallas_call | solution.py:66
  58.1 6.0 %gate_up.7 = (f32[2,64,1024]{2,1,0:T(8,128)S(1)}, bf16[2,64,1024]{2,1,0:T(8,128)(2,1)S(1)}, bf16[512,4096]{1,0:T(8,128)(2,1)S(1)}, bf16[1024,4096]{1,0:T(8,128)(2,1)S(1)}) custom-call(s32[1]{0:T(128)} %bitcast.refs_0_, bf16[128,4096]{1,0:T(8,128)(2,1)S(1)} %pad_maximum_fusion.refs_1_, bf16[4096,512]{1,0:T(8,128)(2,1)S(1)} %get-tuple-element.112.refs_2_, ...), custom_call_target="tpu_custom_call" | custom-call | flops 134217728 | bytes 786432 | tf_op jit(solution)/shard_map/gate_up/pallas_call | solution.py:66
  68.0 5.8 %down.4 = (f32[128,4096]{1,0:T(8,128)S(1)}, bf16[1024,4096]{1,0:T(8,128)(2,1)S(1)}, bf16[1024,4096]{1,0:T(8,128)(2,1)S(1)}) custom-call(s32[1]{0:T(128)} %bitcast.refs_0_, bf16[64,512]{1,0:T(8,128)(2,1)S(1)} %fusion.14.refs_1_, bf16[64,1024]{1,0:T(8,128)(2,1)S(1)} %fusion.6.refs_2_, bf16[64,512]{1,0:T(8,128)(2,1)S(1)} %collective-permute-done.19.refs_3_, ...), custom_call_target="tpu_custom_call" | custom-call | flops 100663296 | bytes 1048576 | tf_op jit(solution)/shard_map/down/pallas_call | solution.py:66
  73.9 1.4 %down.5.refs_4_ = f32[128,4096]{1,0:T(8,128)S(1)} custom-call(s32[1]{0:T(128)} %bitcast.refs_0_, bf16[64,1024]{1,0:T(8,128)(2,1)S(1)} %fusion.8.refs_1_, bf16[64,1024]{1,0:T(8,128)(2,1)S(1)} %collective-permute-done.18.refs_2_, bf16[1024,4096]{1,0:T(8,128)(2,1)S(1)} %get-tuple-element.129.refs_3_, f32[128,4096]{1,0:T(8,128)S(1)} %get-tuple-element.130.refs_4_), custom_call_target="tpu_custom_call" | custom-call | flops 67108864 | tf_op jit(solution)/shard_map/down/pallas_call | solution.py:66
  79.4 1.3 %collective-permute-start.24 = (bf16[32,1536]{1,0:T(8,128)(2,1)S(1)}, bf16[32,1536]{1,0:T(8,128)(2,1)S(1)}, u32[]{:S(2)}, u32[]{:S(2)}) collective-permute-start(bf16[32,1536]{1,0:T(8,128)(2,1)S(1)} %get-tuple-element.137), channel_id=1, source_target_pairs={{0,8},{4,12},{8,0},{12,4},{16,24},{20,28},{24,16},{28,20},{1,9},{5... | collective-permute-start | bytes 294920 | tf_op jit(solution)/shard_map/ppermute | solution.py:278
  80.7 2.9 %collective-permute-start.25 = (bf16[32,1536]{1,0:T(8,128)(2,1)S(1)}, bf16[32,1536]{1,0:T(8,128)(2,1)S(1)}, u32[]{:S(2)}, u32[]{:S(2)}) collective-permute-start(bf16[32,1536]{1,0:T(8,128)(2,1)S(1)} %get-tuple-element.138), channel_id=1, source_target_pairs={{0,16},{4,20},{8,24},{12,28},{16,0},{20,4},{24,8},{28,12},{1,17},{... | collective-permute-start | bytes 294920 | tf_op jit(solution)/shard_map/ppermute | solution.py:278
  83.8 4.1 %collective-permute-done.23 = bf16[64,2560]{1,0:T(8,128)(2,1)S(1)} collective-permute-done((bf16[64,2560]{1,0:T(8,128)(2,1)S(1)}, bf16[64,2560]{1,0:T(8,128)(2,1)S(1)}, u32[]{:S(2)}, u32[]{:S(2)}) %collective-permute-start.23) | collective-permute-done | bytes 327712 | tf_op jit(solution)/shard_map/ppermute | solution.py:275
  89.1 2.4 %collective-permute-start.29 = (bf16[16,2560]{1,0:T(8,128)(2,1)S(1)}, bf16[16,2560]{1,0:T(8,128)(2,1)S(1)}, u32[]{:S(2)}, u32[]{:S(2)}) collective-permute-start(bf16[16,2560]{1,0:T(8,128)(2,1)S(1)} %get-tuple-element.156), channel_id=1, source_target_pairs={{0,24},{4,28},{8,16},{12,20},{16,8},{20,12},{24,0},{28,4},{1,25},{... | collective-permute-start | bytes 245768 | tf_op jit(solution)/shard_map/ppermute | solution.py:278
  93.8 2.4 %collective-permute-done.29 = bf16[16,2560]{1,0:T(8,128)(2,1)S(1)} collective-permute-done((bf16[16,2560]{1,0:T(8,128)(2,1)S(1)}, bf16[16,2560]{1,0:T(8,128)(2,1)S(1)}, u32[]{:S(2)}, u32[]{:S(2)}) %collective-permute-start.29) | collective-permute-done | bytes 81952 | tf_op jit(solution)/shard_map/ppermute | solution.py:278
  96.3 3.4 %collective-permute-done.28 = bf16[16,2560]{1,0:T(8,128)(2,1)S(1)} collective-permute-done((bf16[16,2560]{1,0:T(8,128)(2,1)S(1)}, bf16[16,2560]{1,0:T(8,128)(2,1)S(1)}, u32[]{:S(2)}, u32[]{:S(2)}) %collective-permute-start.28) | collective-permute-done | bytes 81952 | tf_op jit(solution)/shard_map/ppermute | solution.py:278
  101.0 1.4 %collective-permute-start.32 = (bf16[4,4096]{1,0:T(4,128)(2,1)S(1)}, bf16[4,4096]{1,0:T(4,128)(2,1)S(1)}, u32[]{:S(2)}, u32[]{:S(2)}) collective-permute-start(bf16[4,4096]{1,0:T(4,128)(2,1)S(1)} %get-tuple-element.167), channel_id=1, source_target_pairs={{0,2},{1,3},{2,0},{3,1},{4,6},{5,7},{6,4},{7,5},{8,10},{9,11},{10,... | collective-permute-start | bytes 98312 | tf_op jit(solution)/shard_map/ppermute | solution.py:272
  103.6 1.3 %collective-permute-done.32 = bf16[4,4096]{1,0:T(4,128)(2,1)S(1)} collective-permute-done((bf16[4,4096]{1,0:T(4,128)(2,1)S(1)}, bf16[4,4096]{1,0:T(4,128)(2,1)S(1)}, u32[]{:S(2)}, u32[]{:S(2)}) %collective-permute-start.32) | collective-permute-done | bytes 32800 | tf_op jit(solution)/shard_map/ppermute | solution.py:272
  (100 shorter events, 27.7 us)
Async XLA Ops:
  4.5 4.2 %collective-permute-start = (bf16[4,4096]{1,0:T(4,128)(2,1)S(1)}, bf16[4,4096]{1,0:T(4,128)(2,1)S(1)}, u32[]{:S(2)}, u32[]{:S(2)}) collective-permute-start(bf16[4,4096]{1,0:T(4,128)(2,1)S(1)} %get-tuple-element.168), channel_id=1, source_target_pairs={{0,3},{1,2},{2,1},{3,0},{4,7},{5,6},{6,5},{7,4},{8,11},{9,10},{10,... | collective-permute-start | bytes 98312 | tf_op jit(solution)/shard_map/ppermute | solution.py:272
  11.7 6.1 %collective-permute-start.3 = (bf16[16,1536]{1,0:T(8,128)(2,1)S(1)}, bf16[16,1536]{1,0:T(8,128)(2,1)S(1)}, u32[]{:S(2)}, u32[]{:S(2)}) collective-permute-start(bf16[16,1536]{1,0:T(8,128)(2,1)S(1)} %pad_maximum_fusion.6), channel_id=1, source_target_pairs={{0,4},{4,0},{8,12},{12,8},{16,20},{20,16},{24,28},{28,24},{1,5},{5... | collective-permute-start | bytes 147464 | tf_op jit(solution)/shard_map/ppermute | solution.py:275
  13.3 10.4 %collective-permute-start.6 = (bf16[16,2560]{1,0:T(8,128)(2,1)S(1)}, bf16[16,2560]{1,0:T(8,128)(2,1)S(1)}, u32[]{:S(2)}, u32[]{:S(2)}) collective-permute-start(bf16[16,2560]{1,0:T(8,128)(2,1)S(1)} %get-tuple-element.154), channel_id=1, source_target_pairs={{0,24},{4,28},{8,16},{12,20},{16,8},{20,12},{24,0},{28,4},{1,25},{... | collective-permute-start | bytes 245768 | tf_op jit(solution)/shard_map/ppermute | solution.py:278
  17.0 6.8 %collective-permute-start.5 = (bf16[16,2560]{1,0:T(8,128)(2,1)S(1)}, bf16[16,2560]{1,0:T(8,128)(2,1)S(1)}, u32[]{:S(2)}, u32[]{:S(2)}) collective-permute-start(bf16[16,2560]{1,0:T(8,128)(2,1)S(1)} %get-tuple-element.154), channel_id=1, source_target_pairs={{0,16},{4,20},{8,24},{12,28},{16,0},{20,4},{24,8},{28,12},{1,17},{... | collective-permute-start | bytes 245768 | tf_op jit(solution)/shard_map/ppermute | solution.py:278
  17.0 6.8 %collective-permute-start.4 = (bf16[16,2560]{1,0:T(8,128)(2,1)S(1)}, bf16[16,2560]{1,0:T(8,128)(2,1)S(1)}, u32[]{:S(2)}, u32[]{:S(2)}) collective-permute-start(bf16[16,2560]{1,0:T(8,128)(2,1)S(1)} %get-tuple-element.154), channel_id=1, source_target_pairs={{0,8},{4,12},{8,0},{12,4},{16,24},{20,28},{24,16},{28,20},{1,9},{5... | collective-permute-start | bytes 245768 | tf_op jit(solution)/shard_map/ppermute | solution.py:278
  23.8 11.0 %collective-permute-start.9 = (bf16[32,1536]{1,0:T(8,128)(2,1)S(1)}, bf16[32,1536]{1,0:T(8,128)(2,1)S(1)}, u32[]{:S(2)}, u32[]{:S(2)}) collective-permute-start(bf16[32,1536]{1,0:T(8,128)(2,1)S(1)} %pad_maximum_fusion.2.refs_1_), channel_id=1, source_target_pairs={{0,24},{4,28},{8,16},{12,20},{16,8},{20,12},{24,0},{28,4},{1,25},{... | collective-permute-start | bytes 294920 | tf_op jit(solution)/shard_map/ppermute | solution.py:278
  27.5 7.4 %collective-permute-start.8 = (bf16[32,1536]{1,0:T(8,128)(2,1)S(1)}, bf16[32,1536]{1,0:T(8,128)(2,1)S(1)}, u32[]{:S(2)}, u32[]{:S(2)}) collective-permute-start(bf16[32,1536]{1,0:T(8,128)(2,1)S(1)} %pad_maximum_fusion.2.refs_1_), channel_id=1, source_target_pairs={{0,16},{4,20},{8,24},{12,28},{16,0},{20,4},{24,8},{28,12},{1,17},{... | collective-permute-start | bytes 294920 | tf_op jit(solution)/shard_map/ppermute | solution.py:278
  27.5 7.4 %collective-permute-start.7 = (bf16[32,1536]{1,0:T(8,128)(2,1)S(1)}, bf16[32,1536]{1,0:T(8,128)(2,1)S(1)}, u32[]{:S(2)}, u32[]{:S(2)}) collective-permute-start(bf16[32,1536]{1,0:T(8,128)(2,1)S(1)} %pad_maximum_fusion.2.refs_1_), channel_id=1, source_target_pairs={{0,8},{4,12},{8,0},{12,4},{16,24},{20,28},{24,16},{28,20},{1,9},{5... | collective-permute-start | bytes 294920 | tf_op jit(solution)/shard_map/ppermute | solution.py:278
  28.3 7.4 %collective-permute-start.10 = (bf16[64,2560]{1,0:T(8,128)(2,1)S(1)}, bf16[64,2560]{1,0:T(8,128)(2,1)S(1)}, u32[]{:S(2)}, u32[]{:S(2)}) collective-permute-start(bf16[64,2560]{1,0:T(8,128)(2,1)S(1)} %pad_maximum_fusion.1), channel_id=1, source_target_pairs={{0,4},{4,0},{8,12},{12,8},{16,20},{20,16},{24,28},{28,24},{1,5},{5... | collective-permute-start | bytes 983048 | tf_op jit(solution)/shard_map/ppermute | solution.py:275
  38.7 5.6 %collective-permute-start.12 = (bf16[2,64,512]{2,1,0:T(8,128)(2,1)S(1)}, bf16[2,64,512]{2,1,0:T(8,128)(2,1)S(1)}, u32[]{:S(2)}, u32[]{:S(2)}) collective-permute-start(bf16[2,64,512]{2,1,0:T(8,128)(2,1)S(1)} %fusion.9.refs_6_), channel_id=1, source_target_pairs={{0,2},{1,3},{2,0},{3,1},{4,6},{5,7},{6,4},{7,5},{8,10},{9,11},{10,... | collective-permute-start | bytes 393224 | tf_op jit(solution)/shard_map/ppermute | solution.py:272
  45.9 9.1 %collective-permute-start.14 = (bf16[2,64,1024]{2,1,0:T(8,128)(2,1)S(1)}, bf16[2,64,1024]{2,1,0:T(8,128)(2,1)S(1)}, u32[]{:S(2)}, u32[]{:S(2)}) collective-permute-start(bf16[2,64,1024]{2,1,0:T(8,128)(2,1)S(1)} %fusion.refs_6_), channel_id=1, source_target_pairs={{0,2},{1,3},{2,0},{3,1},{4,6},{5,7},{6,4},{7,5},{8,10},{9,11},{10,... | collective-permute-start | bytes 786440 | tf_op jit(solution)/shard_map/ppermute | solution.py:272
  55.2 11.5 %collective-permute-start.19 = (bf16[64,512]{1,0:T(8,128)(2,1)S(1)}, bf16[64,512]{1,0:T(8,128)(2,1)S(1)}, u32[]{:S(2)}, u32[]{:S(2)}) collective-permute-start(bf16[64,512]{1,0:T(8,128)(2,1)S(1)} %fusion.14.refs_1_), channel_id=1, source_target_pairs={{0,1},{1,0},{2,3},{3,2},{4,5},{5,4},{6,7},{7,6},{8,9},{9,8},{10,11... | collective-permute-start | bytes 196616 | tf_op jit(solution)/shard_map/ppermute | solution.py:272
  56.7 8.4 %collective-permute-start.16 = (bf16[2,64,1024]{2,1,0:T(8,128)(2,1)S(1)}, bf16[2,64,1024]{2,1,0:T(8,128)(2,1)S(1)}, u32[]{:S(2)}, u32[]{:S(2)}) collective-permute-start(bf16[2,64,1024]{2,1,0:T(8,128)(2,1)S(1)} %fusion.1.refs_6_), channel_id=1, source_target_pairs={{0,2},{1,3},{2,0},{3,1},{4,6},{5,7},{6,4},{7,5},{8,10},{9,11},{10,... | collective-permute-start | bytes 786440 | tf_op jit(solution)/shard_map/ppermute | solution.py:272
  58.0 8.7 %collective-permute-start.20 = (bf16[64,1024]{1,0:T(8,128)(2,1)S(1)}, bf16[64,1024]{1,0:T(8,128)(2,1)S(1)}, u32[]{:S(2)}, u32[]{:S(2)}) collective-permute-start(bf16[64,1024]{1,0:T(8,128)(2,1)S(1)} %fusion.6.refs_2_), channel_id=1, source_target_pairs={{0,1},{1,0},{2,3},{3,2},{4,5},{5,4},{6,7},{7,6},{8,9},{9,8},{10,11... | collective-permute-start | bytes 393224 | tf_op jit(solution)/shard_map/ppermute | solution.py:272
  66.7 8.5 %collective-permute-start.21 = (bf16[2,64,1024]{2,1,0:T(8,128)(2,1)S(1)}, bf16[2,64,1024]{2,1,0:T(8,128)(2,1)S(1)}, u32[]{:S(2)}, u32[]{:S(2)}) collective-permute-start(bf16[2,64,1024]{2,1,0:T(8,128)(2,1)S(1)} %fusion.2), channel_id=1, source_target_pairs={{0,2},{1,3},{2,0},{3,1},{4,6},{5,7},{6,4},{7,5},{8,10},{9,11},{10,... | collective-permute-start | bytes 786440 | tf_op jit(solution)/shard_map/ppermute | solution.py:272
  67.9 5.9 %collective-permute-start.18 = (bf16[64,1024]{1,0:T(8,128)(2,1)S(1)}, bf16[64,1024]{1,0:T(8,128)(2,1)S(1)}, u32[]{:S(2)}, u32[]{:S(2)}) collective-permute-start(bf16[64,1024]{1,0:T(8,128)(2,1)S(1)} %fusion.8.refs_1_), channel_id=1, source_target_pairs={{0,1},{1,0},{2,3},{3,2},{4,5},{5,4},{6,7},{7,6},{8,9},{9,8},{10,11... | collective-permute-start | bytes 393224 | tf_op jit(solution)/shard_map/ppermute | solution.py:272
  77.9 10.0 %collective-permute-start.23 = (bf16[64,2560]{1,0:T(8,128)(2,1)S(1)}, bf16[64,2560]{1,0:T(8,128)(2,1)S(1)}, u32[]{:S(2)}, u32[]{:S(2)}) collective-permute-start(bf16[64,2560]{1,0:T(8,128)(2,1)S(1)} %get-tuple-element.136.refs_5_), channel_id=1, source_target_pairs={{0,4},{4,0},{8,12},{12,8},{16,20},{20,16},{24,28},{28,24},{1,5},{5... | collective-permute-start | bytes 983048 | tf_op jit(solution)/shard_map/ppermute | solution.py:275
  79.4 12.2 %collective-permute-start.24 = (bf16[32,1536]{1,0:T(8,128)(2,1)S(1)}, bf16[32,1536]{1,0:T(8,128)(2,1)S(1)}, u32[]{:S(2)}, u32[]{:S(2)}) collective-permute-start(bf16[32,1536]{1,0:T(8,128)(2,1)S(1)} %get-tuple-element.137), channel_id=1, source_target_pairs={{0,8},{4,12},{8,0},{12,4},{16,24},{20,28},{24,16},{28,20},{1,9},{5... | collective-permute-start | bytes 294920 | tf_op jit(solution)/shard_map/ppermute | solution.py:278
  80.7 11.4 %collective-permute-start.25 = (bf16[32,1536]{1,0:T(8,128)(2,1)S(1)}, bf16[32,1536]{1,0:T(8,128)(2,1)S(1)}, u32[]{:S(2)}, u32[]{:S(2)}) collective-permute-start(bf16[32,1536]{1,0:T(8,128)(2,1)S(1)} %get-tuple-element.138), channel_id=1, source_target_pairs={{0,16},{4,20},{8,24},{12,28},{16,0},{20,4},{24,8},{28,12},{1,17},{... | collective-permute-start | bytes 294920 | tf_op jit(solution)/shard_map/ppermute | solution.py:278
  83.6 8.5 %collective-permute-start.26 = (bf16[32,1536]{1,0:T(8,128)(2,1)S(1)}, bf16[32,1536]{1,0:T(8,128)(2,1)S(1)}, u32[]{:S(2)}, u32[]{:S(2)}) collective-permute-start(bf16[32,1536]{1,0:T(8,128)(2,1)S(1)} %get-tuple-element.139), channel_id=1, source_target_pairs={{0,24},{4,28},{8,16},{12,20},{16,8},{20,12},{24,0},{28,4},{1,25},{... | collective-permute-start | bytes 294920 | tf_op jit(solution)/shard_map/ppermute | solution.py:278
  88.0 4.6 %collective-permute-start.27 = (bf16[16,2560]{1,0:T(8,128)(2,1)S(1)}, bf16[16,2560]{1,0:T(8,128)(2,1)S(1)}, u32[]{:S(2)}, u32[]{:S(2)}) collective-permute-start(bf16[16,2560]{1,0:T(8,128)(2,1)S(1)} %get-tuple-element.155), channel_id=1, source_target_pairs={{0,8},{4,12},{8,0},{12,4},{16,24},{20,28},{24,16},{28,20},{1,9},{5... | collective-permute-start | bytes 245768 | tf_op jit(solution)/shard_map/ppermute | solution.py:278
  89.1 7.2 %collective-permute-start.29 = (bf16[16,2560]{1,0:T(8,128)(2,1)S(1)}, bf16[16,2560]{1,0:T(8,128)(2,1)S(1)}, u32[]{:S(2)}, u32[]{:S(2)}) collective-permute-start(bf16[16,2560]{1,0:T(8,128)(2,1)S(1)} %get-tuple-element.156), channel_id=1, source_target_pairs={{0,24},{4,28},{8,16},{12,20},{16,8},{20,12},{24,0},{28,4},{1,25},{... | collective-permute-start | bytes 245768 | tf_op jit(solution)/shard_map/ppermute | solution.py:278
  91.5 8.1 %collective-permute-start.28 = (bf16[16,2560]{1,0:T(8,128)(2,1)S(1)}, bf16[16,2560]{1,0:T(8,128)(2,1)S(1)}, u32[]{:S(2)}, u32[]{:S(2)}) collective-permute-start(bf16[16,2560]{1,0:T(8,128)(2,1)S(1)} %get-tuple-element.157), channel_id=1, source_target_pairs={{0,16},{4,20},{8,24},{12,28},{16,0},{20,4},{24,8},{28,12},{1,17},{... | collective-permute-start | bytes 245768 | tf_op jit(solution)/shard_map/ppermute | solution.py:278
  92.7 7.0 %collective-permute-start.30 = (bf16[16,1536]{1,0:T(8,128)(2,1)S(1)}, bf16[16,1536]{1,0:T(8,128)(2,1)S(1)}, u32[]{:S(2)}, u32[]{:S(2)}) collective-permute-start(bf16[16,1536]{1,0:T(8,128)(2,1)S(1)} %slice.181), channel_id=1, source_target_pairs={{0,4},{4,0},{8,12},{12,8},{16,20},{20,16},{24,28},{28,24},{1,5},{5... | collective-permute-start | bytes 147464 | tf_op jit(solution)/shard_map/ppermute | solution.py:275
  (10 other events, 22.9 us)

commit v2 on v1

--- a/solution.py
+++ b/solution.py
@@ -96,7 +96,7 @@
     return done, pieces
 
 
-def attend(lengths, queries, keys, values, new_keys, new_values, resid):
+def attend(lengths, queries, keys, values, new_keys, new_values, resid, gain):
     count, width = queries.shape
     cached = keys.shape[1]
     heads = width // HD
@@ -105,13 +105,14 @@
     inputs = (lengths, queries, keys, new_keys, values, new_values, resid)
 
     def kernel(*refs):
-        slow_refs, refs = refs[: len(inputs)], refs[len(inputs) :]
-        mixed_ref, square_ref, *fast_refs, sems = refs
+        slow_refs, gain_ref, refs = refs[: len(inputs)], refs[len(inputs)], refs[len(inputs) + 1 :]
+        mixed_ref, square_ref, gain_out, *fast_refs, sems = refs
         length_ref, q_ref, k_ref, kn_ref, v_ref, vn_ref, resid_ref = fast_refs
         copies = [
             pltpu.make_async_copy(slow, fast, sems.at[i])
             for i, (slow, fast) in enumerate(zip(slow_refs, fast_refs, strict=True))
         ]
+        copies.append(pltpu.make_async_copy(gain_ref, gain_out, sems.at[len(inputs)]))
         for copy in copies:
             copy.start()
         position = lax.broadcasted_iota(jnp.int32, (heads, cached), 1)
@@ -174,26 +175,37 @@
     fast[0] = pltpu.SMEM(lengths.shape, lengths.dtype)
     return pl.pallas_call(
         kernel,
-        in_specs=[SLOW] * len(inputs),
-        out_specs=[FAST, FAST],
+        in_specs=[SLOW] * (len(inputs) + 1),
+        out_specs=[FAST] * 3,
         out_shape=[
             jax.ShapeDtypeStruct((count, width), F32),
             jax.ShapeDtypeStruct((count, HD), F32),
+            jax.ShapeDtypeStruct(gain.shape, gain.dtype),
         ],
-        scratch_shapes=[*fast, pltpu.SemaphoreType.DMA((len(inputs),))],
+        scratch_shapes=[*fast, pltpu.SemaphoreType.DMA((len(inputs) + 1,))],
         compiler_params=pltpu.CompilerParams(vmem_limit_bytes=16 << 20),
         name="attend",
-    )(*[pltpu.with_memory_space_constraint(x, pltpu.HBM) for x in inputs])
-
-
-def gate_up(core, x, gates, ups, ahead, behind):
-    rows, depth = x.shape
+    )(*[pltpu.with_memory_space_constraint(x, pltpu.HBM) for x in (*inputs, gain)])
+
+
+def gate_up(core, x, gates, ups, ahead, behind, places=None):
+    depth = gates[0].shape[0]
+    pieces = [x] if places is None else x
+    rows = x.shape[0] if places is None else sum(p.size for p in pieces) // depth
     half = rows // 2
+    m = len(pieces)
+    made = [] if places is None else [jax.ShapeDtypeStruct((rows, depth), BF16)]
     n, tile = len(gates), gates[0].shape[1]
 
     def kernel(core_ref, in_refs, out_refs, scratch_refs):
-        x_ref, w_refs = in_refs[0], (in_refs[1 : n + 1], in_refs[n + 1 :])
-        keep_ref, send_ref = out_refs
+        x_ref, w_refs = in_refs[0], (in_refs[m : n + m], in_refs[n + m :])
+        *made_refs, keep_ref, send_ref = out_refs
+        for x_ref in made_refs:
+            for i in range(m):
+                for source, count, row, column in places[i]:
+                    x_ref[row : row + count, column : column + pieces[i].shape[1]] = in_refs[i][
+                        source : source + count, :
+                    ]
         upper = core_ref[0] == 0
         for j in range(n):
             at = slice(j * tile, (j + 1) * tile)
@@ -206,8 +218,9 @@
         kernel,
         "gate_up",
         core,
-        [x, *gates, *ups],
+        [*pieces, *gates, *ups],
         [
+            *made,
             jax.ShapeDtypeStruct((2, half, n * tile), F32),
             jax.ShapeDtypeStruct((2, half, n * tile), BF16),
         ],
@@ -276,13 +289,6 @@
 
     def far_swap(x, slot):
         return lax.ppermute(x, "wide", [(i, i ^ (slot << 1)) for i in range(n_wide)])
-
-    def by_position(first, second):
-        order = []
-        for top in range(2):
-            for side in (first, second):
-                order += side[top * near_far : (top + 1) * near_far]
-        return jnp.concatenate(order, axis=0)
 
     def from_narrow(pieces, am, j):
         out = pieces[j]
@@ -317,7 +323,8 @@
         column_at, row_at, am, core = place
         tile = tile_of(w_gate.shape[1])
         tiles = w_gate.shape[1] // tile
-        chunks = [[0], *[list(range(i, min(i + 2, tiles))) for i in range(1, tiles, 2)]]
+        middle = 1 + tiles // 2
+        chunks = [[0], list(range(1, middle)), list(range(middle, tiles))]
         gates, ups, downs = {}, {}, {}
 
         def gate_up_pieces(which):
@@ -334,17 +341,18 @@
             take(which, pieces)
             return done
 
+        early = chunks[1] + chunks[2][:1]
         def down_pieces(which):
             return [
                 Piece(w_down, chunks[c][0] * tile, len(chunks[c]) * tile, 0, w_down.shape[1])
                 for c in which
             ]
 
-        mixed, mean_square = attend(
-            lengths, queries, key_cache, value_cache, new_keys, new_values, resid
+        mixed, mean_square, gain = attend(
+            lengths, queries, key_cache, value_cache, new_keys, new_values, resid, norm_gain
         )
         normed = (
-            mixed * lax.rsqrt(mean_square[:, :1] + 1e-05) * norm_gain.astype(F32)
+            mixed * lax.rsqrt(mean_square[:, :1] + 1e-05) * gain.astype(F32)
         ).astype(BF16)
         def column_block(x, s):
             return lax.dynamic_slice(x, (jnp.uint32(0), column_at[s]), (own_rows, block))
@@ -352,6 +360,8 @@
         pieces = [column_block(normed, 0)]
         for s in range(1, n_narrow):
             pieces.append(narrow_swap(column_block(normed, s), s))
+        done = bring(chunks[0], [normed])
+        pieces, first_done = lax.optimization_barrier((pieces, done))
         group = jnp.concatenate([from_narrow(pieces, am, j) for j in range(n_narrow)], axis=0)
         group_rows = own_rows * n_narrow
 
@@ -360,27 +370,29 @@
         left, right = group[:, :cut], group[:, cut:]
         pair = jnp.concatenate([left, wide_swap(left)], axis=0)
         far_right = [right] + [far_swap(right, s) for s in range(1, n_far)]
-        first_done = bring([0, 1], [pair])
-        pair = after(pair, far_right)
+        done = bring(early[: len(early) // 2], [pair])
+        pair, far_right, done = lax.optimization_barrier((pair, far_right, done))
+        other = wide_swap(jnp.concatenate(far_right, axis=0))
         far_pairs = [pair] + [far_swap(pair, s) for s in range(1, n_far)]
-        other = wide_swap(jnp.concatenate(far_right, axis=0))
-        second_done = bring([2, 3], [pair])
+        second_done = bring(early[len(early) // 2 :], [pair])
         far_pairs, other, second_done = lax.optimization_barrier((far_pairs, other, second_done))
-        x_left = by_position(
-            [p[:group_rows] for p in far_pairs], [p[group_rows:] for p in far_pairs]
-        )
-        x_right = by_position(
-            far_right,
-            [other[s * group_rows : (s + 1) * group_rows] for s in range(n_far)],
-        )
-        x = jnp.concatenate([x_left, x_right], axis=1)
-
-        plan = [
-            [],
-            gate_up_pieces(chunks[2][1:]),
-            gate_up_pieces(chunks[3]),
-            down_pieces([0, 1]),
+
+        run = near_far * group_rows
+
+        def row_of(far, near):
+            return (2 * (far // near_far) + near) * run + far % near_far * group_rows
+
+        x_pieces = [*far_pairs, *far_right, other]
+        places = [
+            *[
+                [(side * group_rows, group_rows, row_of(s, side), 0) for side in range(2)]
+                for s in range(n_far)
+            ],
+            *[[(0, group_rows, row_of(s, 0), cut)] for s in range(n_far)],
+            [(s * group_rows, group_rows, row_of(s, 1), cut) for s in range(n_far)],
         ]
+
+        plan = [[], gate_up_pieces(chunks[2][1:2]), down_pieces([0])]
         chips, arrived, mine, theirs = [], [], [], []
 
         def finish(c):
@@ -389,54 +401,62 @@
                 total = total + part.astype(F32)
             hidden = (jax.nn.silu(total[0]) * total[1]).astype(BF16)
             mine.append(hidden)
-            theirs.append(narrow_swap(hidden, 1))
 
         for c, which in enumerate(chunks):
-            behind = [sent] if c else [first_done, second_done]
-            (keep, send), pieces = gate_up(
-                core, x, [gates[j] for j in which], [ups[j] for j in which], plan[c], behind
+            behind = [sent] if c else [first_done, done, second_done]
+            if c == 2:
+                bring(chunks[2][2:], [sent])
+            (*made, keep, send), pieces = gate_up(
+                core,
+                x if c else x_pieces,
+                [gates[j] for j in which],
+                [ups[j] for j in which],
+                plan[c],
+                behind,
+                None if c else places,
             )
+            if c == 0:
+                (x,) = made
+            elif c == 1:
+                take(chunks[2][1:2], pieces)
+            else:
+                downs[0] = pieces[0]
             if c == 1:
-                take(chunks[2][1:], pieces)
-            elif c == 2:
-                take(chunks[3], pieces)
-            elif c == 3:
-                downs[0], downs[1] = pieces
-            if c:
                 send, arrived[-1] = lax.optimization_barrier((send, arrived[-1]))
-                finish(c - 1)
             chip = keep + narrow_swap(send, 1).astype(F32)
             sent = chip.astype(BF16)
-            if c == len(chunks) - 1:
-                sent, theirs[:2] = lax.optimization_barrier((sent, theirs[:2]))
+            if c:
+                finish(c - 1)
+            if c > 1:
+                sent, mine[c - 1] = lax.optimization_barrier((sent, mine[c - 1]))
+            if c > 1:
+                sent, theirs[0] = lax.optimization_barrier((sent, theirs[0]))
+            if c:
+                theirs.append(narrow_swap(mine[c - 1], 1))
             chips.append(chip)
             arrived.append([narrow_swap(sent, s) for s in range(2, n_narrow, 2)])
 
         column_tile = tile_of(w_down.shape[1])
         column_tiles = w_down.shape[1] // column_tile
-        sums = None
-        for low, high in ((0, 2), (2, 3)):
-            (sums,), pieces = down(
-                core,
-                mine[low:high],
-                theirs[low:high],
-                sums,
-                [downs[i] for i in range(low, high)],
-                0,
-                column_tiles,
-                column_tile,
-                lambda value: (value,),
-                down_pieces([2, 3]) if low == 0 else [],
-                [],
-            )
-            if low == 0:
-                downs[2], downs[3] = pieces
+        _, (downs[1],) = load(core, down_pieces([1]), [sent])
+        (sums,), (downs[2],) = down(
+            core,
+            mine,
+            theirs,
+            None,
+            [downs[0], downs[1]],
+            0,
+            column_tiles,
+            column_tile,
+            lambda value: (value,),
+            down_pieces([2]),
+            [],
+        )
         sums, arrived[-1] = lax.optimization_barrier((sums, arrived[-1]))
         finish(len(chunks) - 1)
+        theirs.append(narrow_swap(mine[-1], 1))
 
         near_tiles = column_tiles * 5 // 8
-        run = near_far * group_rows
-
         def split_near(value):
             kept = [value[2 * top * run : (2 * top + 1) * run] for top in range(2)]
             sent = [value[(2 * top + 1) * run : (2 * top + 2) * run] for top in range(2)]
@@ -453,10 +473,10 @@
 
         (kept, sent), _ = down(
             core,
-            mine[3:],
-            theirs[3:],
+            mine[2:],
+            theirs[2:],
             sums,
-            [downs[3]],
+            [downs[2]],
             0,
             near_tiles,
             column_tile,
@@ -466,10 +486,10 @@
         )
         far_parts, _ = down(
             core,
-            mine[3:],
-            theirs[3:],
+            mine[2:],
+            theirs[2:],
             sums,
-            [downs[3]],
+            [downs[2]],
             near_tiles,
             column_tiles - near_tiles,
             column_tile,

time: 106 us -> 99.8 us (0.942)
  waiting for transfers between devices: 25.9 us -> 20.3 us
  Pallas kernels: 42.9 us -> 44 us
  other arithmetic: 3.76 us -> 2.66 us
    ppermute x18 -> x15, waiting for transfers between devices: 14.5 us -> 8.75 us  [narrow_swap(): return lax.ppermute(x, 'narrow', [(i, i ^ mask) for i in range(n_narrow)])]
    ppermute x12, waiting for transfers between devices: 6.46 us -> 8.44 us  [far_swap(): return lax.ppermute(x, 'wide', [(i, i ^ slot << 1) for i in range(n_wide)])]
    ppermute x4, waiting for transfers between devices: 4.91 us -> 3.13 us  [wide_swap(): return lax.ppermute(x, 'wide', [(i, i ^ 1) for i in range(n_wide)])]
    pallas_call x10 -> x11, Pallas kernels: 39.6 us -> 40.7 us  [call(): pl.pallas_call(whole, in_specs=[SCALAR, *[FAST] * n_in, *[ANY] * len(behi...]
    ppermute x18 -> x15, starting transfers between devices: 11.1 us -> 10.5 us  [narrow_swap(): return lax.ppermute(x, 'narrow', [(i, i ^ mask) for i in range(n_narrow)])]
  transfers between devices with their start and end apart: 34 -> 31, of which waited for: 16 -> 13; matrix products, arithmetic and copies ran while one was open for 1% -> 1% of each run, Pallas kernels for 35% -> 38%
where the time goes in v2:
time: 99.8 us; the launch traced here: 99.6 us
  Pallas kernels  44 us (44%)
  starting transfers between devices  32 us (32%)
  waiting for transfers between devices  20.3 us (20%)
  other arithmetic  2.66 us (3%)
    pallas_call x11, Pallas kernels, call(): pl.pallas_call(whole, in_specs=[SCALAR, *[FAST] * n_in, *[ANY] * len(behi...  40.7 us
    ppermute x12, starting transfers between devices, far_swap(): return lax.ppermute(x, 'wide', [(i, i ^ slot << 1) for i in range(n_wide)])  16.9 us
    ppermute x15, starting transfers between devices, narrow_swap(): return lax.ppermute(x, 'narrow', [(i, i ^ mask) for i in range(n_narrow)])  10.5 us
    ppermute x15, waiting for transfers between devices, narrow_swap(): return lax.ppermute(x, 'narrow', [(i, i ^ mask) for i in range(n_narrow)])  8.75 us
    ppermute x12, waiting for transfers between devices, far_swap(): return lax.ppermute(x, 'wide', [(i, i ^ slot << 1) for i in range(n_wide)])  8.44 us
    ppermute x4, starting transfers between devices, wide_swap(): return lax.ppermute(x, 'wide', [(i, i ^ 1) for i in range(n_wide)])  4.58 us
    pallas_call x1, Pallas kernels, attend(): pl.pallas_call(kernel, in_specs=[SLOW] * (len(inputs) + 1), out_specs=[FA...  3.33 us
    ppermute x4, waiting for transfers between devices, wide_swap(): return lax.ppermute(x, 'wide', [(i, i ^ 1) for i in range(n_wide)])  3.13 us
  transfers between devices with their start and end apart: 31, of which 13 were waited for; matrix products, arithmetic and copies ran while one was open for 1% of the time, Pallas kernels for 38%

profile of v2, /device:TPU:0, one launch (start us, length us, event | category | flops | bytes accessed | tf_op | source)
XLA Modules:
  0.0 99.6 jit_solution(5382514372933214147)
XLA Ops:
  0.0 3.3 %attend.1 = (f32[4,16384]{1,0:T(4,128)S(1)}, f32[4,128]{1,0:T(4,128)S(1)}, bf16[16384]{0:T(1024)(128)(2,1)S(1)}) custom-call(s32[4]{0:T(128)} %refs_0_.1, bf16[4,16384]{1,0:T(4,128)(2,1)} %refs_1_, bf16[4,192,1024]{2,1,0:T(8,128)(2,1)} %refs_2_.6, bf16[4,1024]{1,0:T(4,128)(2,1)} %refs_3_.5, bf16[4,192,1024]{2,1,0:T(8,128)(2,1)} %refs_4_.1, ...), custom_call_target="tpu_custom_call" | custom-call | tf_op jit(solution)/shard_map/attend/pallas_call | solution.py:176
  3.8 2.4 %collective-permute-start.2 = (bf16[4,4096]{1,0:T(4,128)(2,1)S(1)}, bf16[4,4096]{1,0:T(4,128)(2,1)S(1)}, u32[]{:S(2)}, u32[]{:S(2)}) collective-permute-start(bf16[4,4096]{1,0:T(4,128)(2,1)S(1)} %get-tuple-element.180), channel_id=1, source_target_pairs={{0,3},{1,2},{2,1},{3,0},{4,7},{5,6},{6,5},{7,4},{8,11},{9,10},{10,... | collective-permute-start | bytes 98312 | tf_op jit(solution)/shard_map/ppermute | solution.py:285
  6.9 3.5 %load.5 = (s32[8,128]{1,0:T(8,128)S(1)}, bf16[4096,512]{1,0:T(8,128)(2,1)S(1)}, bf16[4096,512]{1,0:T(8,128)(2,1)S(1)}) custom-call(s32[1]{0:T(128)} %bitcast.refs_0_, bf16[4,16384]{1,0:T(4,128)(2,1)S(1)} %multiply_convert_fusion.refs_1_, bf16[4096,3584]{1,0:T(8,128)(2,1)} %refs_2_.10, bf16[4096,3584]{1,0:T(8,128)(2,1)} %refs_3_.9), custom_call_target="tpu_custom_call" | custom-call | bytes 524288 | tf_op jit(solution)/shard_map/load/pallas_call | solution.py:66
  10.6 1.8 %collective-permute-start.3 = (bf16[16,1536]{1,0:T(8,128)(2,1)S(1)}, bf16[16,1536]{1,0:T(8,128)(2,1)S(1)}, u32[]{:S(2)}, u32[]{:S(2)}) collective-permute-start(bf16[16,1536]{1,0:T(8,128)(2,1)S(1)} %pad_maximum_fusion.5), channel_id=1, source_target_pairs={{0,4},{4,0},{8,12},{12,8},{16,20},{20,16},{24,28},{28,24},{1,5},{5... | collective-permute-start | bytes 147464 | tf_op jit(solution)/shard_map/ppermute | solution.py:288
  12.4 3.7 %collective-permute-start.6 = (bf16[16,2560]{1,0:T(8,128)(2,1)S(1)}, bf16[16,2560]{1,0:T(8,128)(2,1)S(1)}, u32[]{:S(2)}, u32[]{:S(2)}) collective-permute-start(bf16[16,2560]{1,0:T(8,128)(2,1)S(1)} %pad_maximum_fusion.2.refs_5_), channel_id=1, source_target_pairs={{0,24},{4,28},{8,16},{12,20},{16,8},{20,12},{24,0},{28,4},{1,25},{... | collective-permute-start | bytes 245768 | tf_op jit(solution)/shard_map/ppermute | solution.py:291
  16.9 6.0 %load.6 = (s32[8,128]{1,0:T(8,128)S(1)}, bf16[4096,512]{1,0:T(8,128)(2,1)S(1)}, bf16[4096,512]{1,0:T(8,128)(2,1)S(1)}, bf16[4096,512]{1,0:T(8,128)(2,1)S(1)}, bf16[4096,512]{1,0:T(8,128)(2,1)S(1)}) custom-call(s32[1]{0:T(128)} %bitcast.refs_0_, bf16[32,1536]{1,0:T(8,128)(2,1)S(1)} %pad_maximum_fusion.1.refs_1_, bf16[4096,3584]{1,0:T(8,128)(2,1)} %refs_2_.10, ...), custom_call_target="tpu_custom_call" | custom-call | bytes 1048576 | tf_op jit(solution)/shard_map/load/pallas_call | solution.py:66
  23.7 3.4 %collective-permute-start.9 = (bf16[32,1536]{1,0:T(8,128)(2,1)S(1)}, bf16[32,1536]{1,0:T(8,128)(2,1)S(1)}, u32[]{:S(2)}, u32[]{:S(2)}) collective-permute-start(bf16[32,1536]{1,0:T(8,128)(2,1)S(1)} %pad_maximum_fusion.1.refs_1_), channel_id=1, source_target_pairs={{0,24},{4,28},{8,16},{12,20},{16,8},{20,12},{24,0},{28,4},{1,25},{... | collective-permute-start | bytes 294920 | tf_op jit(solution)/shard_map/ppermute | solution.py:291
  28.1 5.9 %load.7 = (s32[8,128]{1,0:T(8,128)S(1)}, bf16[4096,512]{1,0:T(8,128)(2,1)S(1)}, bf16[4096,512]{1,0:T(8,128)(2,1)S(1)}, bf16[4096,512]{1,0:T(8,128)(2,1)S(1)}, bf16[4096,512]{1,0:T(8,128)(2,1)S(1)}) custom-call(s32[1]{0:T(128)} %bitcast.refs_0_, bf16[32,1536]{1,0:T(8,128)(2,1)S(1)} %pad_maximum_fusion.1.refs_1_, bf16[4096,3584]{1,0:T(8,128)(2,1)} %refs_2_.10, ...), custom_call_target="tpu_custom_call" | custom-call | bytes 1048576 | tf_op jit(solution)/shard_map/load/pallas_call | solution.py:66
  34.5 1.3 %gate_up.3 = (bf16[128,4096]{1,0:T(8,128)(2,1)S(1)}, f32[2,64,512]{2,1,0:T(8,128)S(1)}, bf16[2,64,512]{2,1,0:T(8,128)(2,1)S(1)}) custom-call(s32[1]{0:T(128)} %bitcast.refs_0_, bf16[32,1536]{1,0:T(8,128)(2,1)S(1)} %pad_maximum_fusion.1.refs_1_, bf16[32,1536]{1,0:T(8,128)(2,1)S(1)} %collective-permute-done.7.refs_2_, ...), custom_call_target="tpu_custom_call" | custom-call | flops 67108864 | tf_op jit(solution)/shard_map/gate_up/pallas_call | solution.py:66
  37.3 1.6 %collective-permute-start.12 = (bf16[2,64,512]{2,1,0:T(8,128)(2,1)S(1)}, bf16[2,64,512]{2,1,0:T(8,128)(2,1)S(1)}, u32[]{:S(2)}, u32[]{:S(2)}) collective-permute-start(bf16[2,64,512]{2,1,0:T(8,128)(2,1)S(1)} %fusion.6.refs_8_), channel_id=1, source_target_pairs={{0,2},{1,3},{2,0},{3,1},{4,6},{5,7},{6,4},{7,5},{8,10},{9,11},{10,... | collective-permute-start | bytes 393224 | tf_op jit(solution)/shard_map/ppermute | solution.py:285
  38.9 4.4 %gate_up.4 = (f32[2,64,1536]{2,1,0:T(8,128)S(1)}, bf16[2,64,1536]{2,1,0:T(8,128)(2,1)S(1)}, bf16[4096,512]{1,0:T(8,128)(2,1)S(1)}, bf16[4096,512]{1,0:T(8,128)(2,1)S(1)}) custom-call(s32[1]{0:T(128)} %bitcast.refs_0_, bf16[128,4096]{1,0:T(8,128)(2,1)S(1)} %get-tuple-element.118.refs_1_, bf16[4096,512]{1,0:T(8,128)(2,1)S(1)} %get-tuple-element.120.refs_2_, ...), custom_call_target="tpu_custom_call" | custom-call | flops 201326592 | bytes 524288 | tf_op jit(solution)/shard_map/gate_up/pallas_call | solution.py:66
  43.4 1.7 %collective-permute-done.13 = bf16[2,64,1536]{2,1,0:T(8,128)(2,1)S(1)} collective-permute-done((bf16[2,64,1536]{2,1,0:T(8,128)(2,1)S(1)}, bf16[2,64,1536]{2,1,0:T(8,128)(2,1)S(1)}, u32[]{:S(2)}, u32[]{:S(2)}) %collective-permute-start.13) | collective-permute-done | bytes 393248 | tf_op jit(solution)/shard_map/ppermute | solution.py:285
  46.5 4.1 %load.8 = (s32[8,128]{1,0:T(8,128)}, bf16[4096,512]{1,0:T(8,128)(2,1)S(1)}, bf16[4096,512]{1,0:T(8,128)(2,1)S(1)}) custom-call(s32[1]{0:T(128)} %bitcast.refs_0_, bf16[2,64,1536]{2,1,0:T(8,128)(2,1)S(1)} %fusion.refs_1_.refs_8_, bf16[4096,3584]{1,0:T(8,128)(2,1)} %refs_2_.10, bf16[4096,3584]{1,0:T(8,128)(2,1)} %refs_3_.9), custom_call_target="tpu_custom_call" | custom-call | bytes 524288 | tf_op jit(solution)/shard_map/load/pallas_call | solution.py:66
  50.6 3.5 %gate_up.5 = (f32[2,64,1536]{2,1,0:T(8,128)S(1)}, bf16[2,64,1536]{2,1,0:T(8,128)(2,1)S(1)}, bf16[512,4096]{1,0:T(8,128)(2,1)S(1)}) custom-call(s32[1]{0:T(128)} %bitcast.refs_0_, bf16[128,4096]{1,0:T(8,128)(2,1)S(1)} %get-tuple-element.118.refs_1_, bf16[4096,512]{1,0:T(8,128)(2,1)S(1)} %get-tuple-element.119.refs_2_, ...), custom_call_target="tpu_custom_call" | custom-call | flops 201326592 | bytes 262144 | tf_op jit(solution)/shard_map/gate_up/pallas_call | solution.py:66
  54.7 1.8 %collective-permute-done.15 = bf16[2,64,1536]{2,1,0:T(8,128)(2,1)S(1)} collective-permute-done((bf16[2,64,1536]{2,1,0:T(8,128)(2,1)S(1)}, bf16[2,64,1536]{2,1,0:T(8,128)(2,1)S(1)}, u32[]{:S(2)}, u32[]{:S(2)}) %collective-permute-start.15) | collective-permute-done | bytes 393248 | tf_op jit(solution)/shard_map/ppermute | solution.py:285
  57.9 5.2 %load.9 = (s32[8,128]{1,0:T(8,128)}, bf16[1536,4096]{1,0:T(8,128)(2,1)S(1)}) custom-call(s32[1]{0:T(128)} %bitcast.refs_0_, bf16[2,64,1536]{2,1,0:T(8,128)(2,1)S(1)} %fusion.1.refs_1_, bf16[3584,4096]{1,0:T(8,128)(2,1)} %refs_7_.3), custom_call_target="tpu_custom_call" | custom-call | bytes 786432 | tf_op jit(solution)/shard_map/load/pallas_call | solution.py:66
  63.1 4.6 %down.3 = (f32[128,4096]{1,0:T(8,128)S(1)}, bf16[1536,4096]{1,0:T(8,128)(2,1)S(1)}) custom-call(s32[1]{0:T(128)} %bitcast.refs_0_, bf16[64,512]{1,0:T(8,128)(2,1)S(1)} %fusion.11.refs_1_, bf16[64,1536]{1,0:T(8,128)(2,1)S(1)} %fusion.5.refs_2_, bf16[64,512]{1,0:T(8,128)(2,1)S(1)} %collective-permute-done.16.refs_3_, ...), custom_call_target="tpu_custom_call" | custom-call | flops 134217728 | bytes 786432 | tf_op jit(solution)/shard_map/down/pallas_call | solution.py:66
  70.9 1.6 %collective-permute-start.20 = (bf16[64,2560]{1,0:T(8,128)(2,1)S(1)}, bf16[64,2560]{1,0:T(8,128)(2,1)S(1)}, u32[]{:S(2)}, u32[]{:S(2)}) collective-permute-start(bf16[64,2560]{1,0:T(8,128)(2,1)S(1)} %get-tuple-element.150.refs_5_), channel_id=1, source_target_pairs={{0,4},{4,0},{8,12},{12,8},{16,20},{20,16},{24,28},{28,24},{1,5},{5... | collective-permute-start | bytes 983048 | tf_op jit(solution)/shard_map/ppermute | solution.py:288
  74.1 2.9 %collective-permute-start.22 = (bf16[32,1536]{1,0:T(8,128)(2,1)S(1)}, bf16[32,1536]{1,0:T(8,128)(2,1)S(1)}, u32[]{:S(2)}, u32[]{:S(2)}) collective-permute-start(bf16[32,1536]{1,0:T(8,128)(2,1)S(1)} %get-tuple-element.152), channel_id=1, source_target_pairs={{0,16},{4,20},{8,24},{12,28},{16,0},{20,4},{24,8},{28,12},{1,17},{... | collective-permute-start | bytes 294920 | tf_op jit(solution)/shard_map/ppermute | solution.py:291
  77.9 3.1 %collective-permute-done.20 = bf16[64,2560]{1,0:T(8,128)(2,1)S(1)} collective-permute-done((bf16[64,2560]{1,0:T(8,128)(2,1)S(1)}, bf16[64,2560]{1,0:T(8,128)(2,1)S(1)}, u32[]{:S(2)}, u32[]{:S(2)}) %collective-permute-start.20) | collective-permute-done | bytes 327712 | tf_op jit(solution)/shard_map/ppermute | solution.py:288
  81.8 2.5 %collective-permute-start.26 = (bf16[16,2560]{1,0:T(8,128)(2,1)S(1)}, bf16[16,2560]{1,0:T(8,128)(2,1)S(1)}, u32[]{:S(2)}, u32[]{:S(2)}) collective-permute-start(bf16[16,2560]{1,0:T(8,128)(2,1)S(1)} %get-tuple-element.168), channel_id=1, source_target_pairs={{0,24},{4,28},{8,16},{12,20},{16,8},{20,12},{24,0},{28,4},{1,25},{... | collective-permute-start | bytes 245768 | tf_op jit(solution)/shard_map/ppermute | solution.py:291
  84.9 2.1 %collective-permute-done.24 = bf16[16,2560]{1,0:T(8,128)(2,1)S(1)} collective-permute-done((bf16[16,2560]{1,0:T(8,128)(2,1)S(1)}, bf16[16,2560]{1,0:T(8,128)(2,1)S(1)}, u32[]{:S(2)}, u32[]{:S(2)}) %collective-permute-start.24) | collective-permute-done | bytes 81952 | tf_op jit(solution)/shard_map/ppermute | solution.py:291
  88.9 4.2 %collective-permute-done.25 = bf16[16,2560]{1,0:T(8,128)(2,1)S(1)} collective-permute-done((bf16[16,2560]{1,0:T(8,128)(2,1)S(1)}, bf16[16,2560]{1,0:T(8,128)(2,1)S(1)}, u32[]{:S(2)}, u32[]{:S(2)}) %collective-permute-start.25) | collective-permute-done | bytes 81952 | tf_op jit(solution)/shard_map/ppermute | solution.py:291
  97.1 1.6 %collective-permute-done.29 = bf16[4,4096]{1,0:T(4,128)(2,1)S(1)} collective-permute-done((bf16[4,4096]{1,0:T(4,128)(2,1)S(1)}, bf16[4,4096]{1,0:T(4,128)(2,1)S(1)}, u32[]{:S(2)}, u32[]{:S(2)}) %collective-permute-start.29) | collective-permute-done | bytes 32800 | tf_op jit(solution)/shard_map/ppermute | solution.py:285
  (78 shorter events, 22.9 us)
Async XLA Ops:
  3.8 6.6 %collective-permute-start.2 = (bf16[4,4096]{1,0:T(4,128)(2,1)S(1)}, bf16[4,4096]{1,0:T(4,128)(2,1)S(1)}, u32[]{:S(2)}, u32[]{:S(2)}) collective-permute-start(bf16[4,4096]{1,0:T(4,128)(2,1)S(1)} %get-tuple-element.180), channel_id=1, source_target_pairs={{0,3},{1,2},{2,1},{3,0},{4,7},{5,6},{6,5},{7,4},{8,11},{9,10},{10,... | collective-permute-start | bytes 98312 | tf_op jit(solution)/shard_map/ppermute | solution.py:285
  6.2 4.2 %collective-permute-start.1 = (bf16[4,4096]{1,0:T(4,128)(2,1)S(1)}, bf16[4,4096]{1,0:T(4,128)(2,1)S(1)}, u32[]{:S(2)}, u32[]{:S(2)}) collective-permute-start(bf16[4,4096]{1,0:T(4,128)(2,1)S(1)} %get-tuple-element.181), channel_id=1, source_target_pairs={{0,2},{1,3},{2,0},{3,1},{4,6},{5,7},{6,4},{7,5},{8,10},{9,11},{10,... | collective-permute-start | bytes 98312 | tf_op jit(solution)/shard_map/ppermute | solution.py:285
  10.6 6.3 %collective-permute-start.3 = (bf16[16,1536]{1,0:T(8,128)(2,1)S(1)}, bf16[16,1536]{1,0:T(8,128)(2,1)S(1)}, u32[]{:S(2)}, u32[]{:S(2)}) collective-permute-start(bf16[16,1536]{1,0:T(8,128)(2,1)S(1)} %pad_maximum_fusion.5), channel_id=1, source_target_pairs={{0,4},{4,0},{8,12},{12,8},{16,20},{20,16},{24,28},{28,24},{1,5},{5... | collective-permute-start | bytes 147464 | tf_op jit(solution)/shard_map/ppermute | solution.py:288
  12.4 10.4 %collective-permute-start.6 = (bf16[16,2560]{1,0:T(8,128)(2,1)S(1)}, bf16[16,2560]{1,0:T(8,128)(2,1)S(1)}, u32[]{:S(2)}, u32[]{:S(2)}) collective-permute-start(bf16[16,2560]{1,0:T(8,128)(2,1)S(1)} %pad_maximum_fusion.2.refs_5_), channel_id=1, source_target_pairs={{0,24},{4,28},{8,16},{12,20},{16,8},{20,12},{24,0},{28,4},{1,25},{... | collective-permute-start | bytes 245768 | tf_op jit(solution)/shard_map/ppermute | solution.py:291
  16.1 7.0 %collective-permute-start.5 = (bf16[16,2560]{1,0:T(8,128)(2,1)S(1)}, bf16[16,2560]{1,0:T(8,128)(2,1)S(1)}, u32[]{:S(2)}, u32[]{:S(2)}) collective-permute-start(bf16[16,2560]{1,0:T(8,128)(2,1)S(1)} %pad_maximum_fusion.2.refs_5_), channel_id=1, source_target_pairs={{0,16},{4,20},{8,24},{12,28},{16,0},{20,4},{24,8},{28,12},{1,17},{... | collective-permute-start | bytes 245768 | tf_op jit(solution)/shard_map/ppermute | solution.py:291
  16.1 7.0 %collective-permute-start.4 = (bf16[16,2560]{1,0:T(8,128)(2,1)S(1)}, bf16[16,2560]{1,0:T(8,128)(2,1)S(1)}, u32[]{:S(2)}, u32[]{:S(2)}) collective-permute-start(bf16[16,2560]{1,0:T(8,128)(2,1)S(1)} %pad_maximum_fusion.2.refs_5_), channel_id=1, source_target_pairs={{0,8},{4,12},{8,0},{12,4},{16,24},{20,28},{24,16},{28,20},{1,9},{5... | collective-permute-start | bytes 245768 | tf_op jit(solution)/shard_map/ppermute | solution.py:291
  23.1 11.4 %collective-permute-start.10 = (bf16[64,2560]{1,0:T(8,128)(2,1)S(1)}, bf16[64,2560]{1,0:T(8,128)(2,1)S(1)}, u32[]{:S(2)}, u32[]{:S(2)}) collective-permute-start(bf16[64,2560]{1,0:T(8,128)(2,1)S(1)} %pad_maximum_fusion), channel_id=1, source_target_pairs={{0,4},{4,0},{8,12},{12,8},{16,20},{20,16},{24,28},{28,24},{1,5},{5... | collective-permute-start | bytes 983048 | tf_op jit(solution)/shard_map/ppermute | solution.py:288
  23.7 10.3 %collective-permute-start.9 = (bf16[32,1536]{1,0:T(8,128)(2,1)S(1)}, bf16[32,1536]{1,0:T(8,128)(2,1)S(1)}, u32[]{:S(2)}, u32[]{:S(2)}) collective-permute-start(bf16[32,1536]{1,0:T(8,128)(2,1)S(1)} %pad_maximum_fusion.1.refs_1_), channel_id=1, source_target_pairs={{0,24},{4,28},{8,16},{12,20},{16,8},{20,12},{24,0},{28,4},{1,25},{... | collective-permute-start | bytes 294920 | tf_op jit(solution)/shard_map/ppermute | solution.py:291
  27.1 7.3 %collective-permute-start.8 = (bf16[32,1536]{1,0:T(8,128)(2,1)S(1)}, bf16[32,1536]{1,0:T(8,128)(2,1)S(1)}, u32[]{:S(2)}, u32[]{:S(2)}) collective-permute-start(bf16[32,1536]{1,0:T(8,128)(2,1)S(1)} %pad_maximum_fusion.1.refs_1_), channel_id=1, source_target_pairs={{0,16},{4,20},{8,24},{12,28},{16,0},{20,4},{24,8},{28,12},{1,17},{... | collective-permute-start | bytes 294920 | tf_op jit(solution)/shard_map/ppermute | solution.py:291
  27.1 7.3 %collective-permute-start.7 = (bf16[32,1536]{1,0:T(8,128)(2,1)S(1)}, bf16[32,1536]{1,0:T(8,128)(2,1)S(1)}, u32[]{:S(2)}, u32[]{:S(2)}) collective-permute-start(bf16[32,1536]{1,0:T(8,128)(2,1)S(1)} %pad_maximum_fusion.1.refs_1_), channel_id=1, source_target_pairs={{0,8},{4,12},{8,0},{12,4},{16,24},{20,28},{24,16},{28,20},{1,9},{5... | collective-permute-start | bytes 294920 | tf_op jit(solution)/shard_map/ppermute | solution.py:291
  37.3 6.0 %collective-permute-start.12 = (bf16[2,64,512]{2,1,0:T(8,128)(2,1)S(1)}, bf16[2,64,512]{2,1,0:T(8,128)(2,1)S(1)}, u32[]{:S(2)}, u32[]{:S(2)}) collective-permute-start(bf16[2,64,512]{2,1,0:T(8,128)(2,1)S(1)} %fusion.6.refs_8_), channel_id=1, source_target_pairs={{0,2},{1,3},{2,0},{3,1},{4,6},{5,7},{6,4},{7,5},{8,10},{9,11},{10,... | collective-permute-start | bytes 393224 | tf_op jit(solution)/shard_map/ppermute | solution.py:285
  45.2 11.2 %collective-permute-start.15 = (bf16[2,64,1536]{2,1,0:T(8,128)(2,1)S(1)}, bf16[2,64,1536]{2,1,0:T(8,128)(2,1)S(1)}, u32[]{:S(2)}, u32[]{:S(2)}) collective-permute-start(bf16[2,64,1536]{2,1,0:T(8,128)(2,1)S(1)} %fusion.refs_1_.refs_8_), channel_id=1, source_target_pairs={{0,2},{1,3},{2,0},{3,1},{4,6},{5,7},{6,4},{7,5},{8,10},{9,11},{10,... | collective-permute-start | bytes 1179656 | tf_op jit(solution)/shard_map/ppermute | solution.py:285
  46.4 10.4 %collective-permute-start.16 = (bf16[64,512]{1,0:T(8,128)(2,1)S(1)}, bf16[64,512]{1,0:T(8,128)(2,1)S(1)}, u32[]{:S(2)}, u32[]{:S(2)}) collective-permute-start(bf16[64,512]{1,0:T(8,128)(2,1)S(1)} %fusion.11.refs_1_), channel_id=1, source_target_pairs={{0,1},{1,0},{2,3},{3,2},{4,5},{5,4},{6,7},{7,6},{8,9},{9,8},{10,11... | collective-permute-start | bytes 196616 | tf_op jit(solution)/shard_map/ppermute | solution.py:285
  56.8 10.9 %collective-permute-start.18 = (bf16[2,64,1536]{2,1,0:T(8,128)(2,1)S(1)}, bf16[2,64,1536]{2,1,0:T(8,128)(2,1)S(1)}, u32[]{:S(2)}, u32[]{:S(2)}) collective-permute-start(bf16[2,64,1536]{2,1,0:T(8,128)(2,1)S(1)} %fusion.1.refs_1_), channel_id=1, source_target_pairs={{0,2},{1,3},{2,0},{3,1},{4,6},{5,7},{6,4},{7,5},{8,10},{9,11},{10,... | collective-permute-start | bytes 1179656 | tf_op jit(solution)/shard_map/ppermute | solution.py:285
  57.9 5.2 %collective-permute-start.17 = (bf16[64,1536]{1,0:T(8,128)(2,1)S(1)}, bf16[64,1536]{1,0:T(8,128)(2,1)S(1)}, u32[]{:S(2)}, u32[]{:S(2)}) collective-permute-start(bf16[64,1536]{1,0:T(8,128)(2,1)S(1)} %fusion.5.refs_2_), channel_id=1, source_target_pairs={{0,1},{1,0},{2,3},{3,2},{4,5},{5,4},{6,7},{7,6},{8,9},{9,8},{10,11... | collective-permute-start | bytes 589832 | tf_op jit(solution)/shard_map/ppermute | solution.py:285
  70.9 10.1 %collective-permute-start.20 = (bf16[64,2560]{1,0:T(8,128)(2,1)S(1)}, bf16[64,2560]{1,0:T(8,128)(2,1)S(1)}, u32[]{:S(2)}, u32[]{:S(2)}) collective-permute-start(bf16[64,2560]{1,0:T(8,128)(2,1)S(1)} %get-tuple-element.150.refs_5_), channel_id=1, source_target_pairs={{0,4},{4,0},{8,12},{12,8},{16,20},{20,16},{24,28},{28,24},{1,5},{5... | collective-permute-start | bytes 983048 | tf_op jit(solution)/shard_map/ppermute | solution.py:288
  73.4 10.8 %collective-permute-start.21 = (bf16[32,1536]{1,0:T(8,128)(2,1)S(1)}, bf16[32,1536]{1,0:T(8,128)(2,1)S(1)}, u32[]{:S(2)}, u32[]{:S(2)}) collective-permute-start(bf16[32,1536]{1,0:T(8,128)(2,1)S(1)} %get-tuple-element.151), channel_id=1, source_target_pairs={{0,8},{4,12},{8,0},{12,4},{16,24},{20,28},{24,16},{28,20},{1,9},{5... | collective-permute-start | bytes 294920 | tf_op jit(solution)/shard_map/ppermute | solution.py:291
  74.1 10.8 %collective-permute-start.22 = (bf16[32,1536]{1,0:T(8,128)(2,1)S(1)}, bf16[32,1536]{1,0:T(8,128)(2,1)S(1)}, u32[]{:S(2)}, u32[]{:S(2)}) collective-permute-start(bf16[32,1536]{1,0:T(8,128)(2,1)S(1)} %get-tuple-element.152), channel_id=1, source_target_pairs={{0,16},{4,20},{8,24},{12,28},{16,0},{20,4},{24,8},{28,12},{1,17},{... | collective-permute-start | bytes 294920 | tf_op jit(solution)/shard_map/ppermute | solution.py:291
  77.0 7.9 %collective-permute-start.23 = (bf16[32,1536]{1,0:T(8,128)(2,1)S(1)}, bf16[32,1536]{1,0:T(8,128)(2,1)S(1)}, u32[]{:S(2)}, u32[]{:S(2)}) collective-permute-start(bf16[32,1536]{1,0:T(8,128)(2,1)S(1)} %get-tuple-element.153), channel_id=1, source_target_pairs={{0,24},{4,28},{8,16},{12,20},{16,8},{20,12},{24,0},{28,4},{1,25},{... | collective-permute-start | bytes 294920 | tf_op jit(solution)/shard_map/ppermute | solution.py:291
  81.1 5.9 %collective-permute-start.24 = (bf16[16,2560]{1,0:T(8,128)(2,1)S(1)}, bf16[16,2560]{1,0:T(8,128)(2,1)S(1)}, u32[]{:S(2)}, u32[]{:S(2)}) collective-permute-start(bf16[16,2560]{1,0:T(8,128)(2,1)S(1)} %get-tuple-element.167), channel_id=1, source_target_pairs={{0,8},{4,12},{8,0},{12,4},{16,24},{20,28},{24,16},{28,20},{1,9},{5... | collective-permute-start | bytes 245768 | tf_op jit(solution)/shard_map/ppermute | solution.py:291
  81.8 7.2 %collective-permute-start.26 = (bf16[16,2560]{1,0:T(8,128)(2,1)S(1)}, bf16[16,2560]{1,0:T(8,128)(2,1)S(1)}, u32[]{:S(2)}, u32[]{:S(2)}) collective-permute-start(bf16[16,2560]{1,0:T(8,128)(2,1)S(1)} %get-tuple-element.168), channel_id=1, source_target_pairs={{0,24},{4,28},{8,16},{12,20},{16,8},{20,12},{24,0},{28,4},{1,25},{... | collective-permute-start | bytes 245768 | tf_op jit(solution)/shard_map/ppermute | solution.py:291
  84.2 8.9 %collective-permute-start.25 = (bf16[16,2560]{1,0:T(8,128)(2,1)S(1)}, bf16[16,2560]{1,0:T(8,128)(2,1)S(1)}, u32[]{:S(2)}, u32[]{:S(2)}) collective-permute-start(bf16[16,2560]{1,0:T(8,128)(2,1)S(1)} %get-tuple-element.169), channel_id=1, source_target_pairs={{0,16},{4,20},{8,24},{12,28},{16,0},{20,4},{24,8},{28,12},{1,17},{... | collective-permute-start | bytes 245768 | tf_op jit(solution)/shard_map/ppermute | solution.py:291
  87.0 6.2 %collective-permute-start.27 = (bf16[16,1536]{1,0:T(8,128)(2,1)S(1)}, bf16[16,1536]{1,0:T(8,128)(2,1)S(1)}, u32[]{:S(2)}, u32[]{:S(2)}) collective-permute-start(bf16[16,1536]{1,0:T(8,128)(2,1)S(1)} %slice.109), channel_id=1, source_target_pairs={{0,4},{4,0},{8,12},{12,8},{16,20},{20,16},{24,28},{28,24},{1,5},{5... | collective-permute-start | bytes 147464 | tf_op jit(solution)/shard_map/ppermute | solution.py:288
  94.7 3.9 %collective-permute-start.29 = (bf16[4,4096]{1,0:T(4,128)(2,1)S(1)}, bf16[4,4096]{1,0:T(4,128)(2,1)S(1)}, u32[]{:S(2)}, u32[]{:S(2)}) collective-permute-start(bf16[4,4096]{1,0:T(4,128)(2,1)S(1)} %get-tuple-element.175), channel_id=1, source_target_pairs={{0,2},{1,3},{2,0},{3,1},{4,6},{5,7},{6,4},{7,5},{8,10},{9,11},{10,... | collective-permute-start | bytes 98312 | tf_op jit(solution)/shard_map/ppermute | solution.py:285
  (7 other events, 16.5 us)

commit v3 on v2

--- a/solution.py
+++ b/solution.py
@@ -35,13 +35,15 @@
         self.row, self.rows, self.column, self.columns = row, rows, column, columns
 
 
-def call(kernel, name, flags, inputs, outputs, ahead, scratch, flops, behind):
+def call(kernel, name, flags, inputs, outputs, ahead, scratch, flops, behind, late=()):
+    moving = (*late, *ahead)
     weights = []
-    for piece in ahead:
+    for piece in moving:
         if not any(piece.weight is w for w in weights):
             weights.append(piece.weight)
-    source = [next(i for i, w in enumerate(weights) if w is p.weight) for p in ahead]
+    source = [next(i for i, w in enumerate(weights) if w is p.weight) for p in moving]
     n_in, n_w, n_out, n_a = len(inputs), len(weights), len(outputs), len(ahead)
+    n_late = len(late)
 
     def whole(*refs):
         flag_ref, refs = refs[0], refs[1:]
@@ -49,27 +51,37 @@
         weight_refs, refs = refs[:n_w], refs[n_w:]
         out_refs, refs = refs[:n_out], refs[n_out:]
         ahead_refs, refs = refs[:n_a], refs[n_a:]
-        sems, scratch_refs = refs[0], refs[1:]
+        sems, refs = refs[0], refs[1:]
+        late_refs, scratch_refs = refs[:n_late], refs[n_late:]
+        targets = (*late_refs, *ahead_refs)
         copies = []
-        for i, piece in enumerate(ahead):
+        for i, piece in enumerate(moving):
             view = weight_refs[source[i]].at[
                 pl.ds(piece.row, piece.rows), pl.ds(piece.column, piece.columns)
             ]
-            copies.append(pltpu.make_async_copy(view, ahead_refs[i], sems.at[i]))
+            copies.append(pltpu.make_async_copy(view, targets[i], sems.at[i]))
         for copy in copies:
             copy.start()
-        kernel(flag_ref, in_refs, out_refs, scratch_refs)
-        for copy in copies:
+        if late:
+            kernel(flag_ref, in_refs, out_refs, scratch_refs, late_refs, copies[:n_late])
+        else:
+            kernel(flag_ref, in_refs, out_refs, scratch_refs)
+        for copy in copies[n_late:]:
             copy.wait()
 
-    moved = sum(2 * p.rows * p.columns for p in ahead)
+    moved = sum(2 * p.rows * p.columns for p in moving)
+    own = sum(2 * p.rows * p.columns for p in late)
     result = pl.pallas_call(
         whole,
         in_specs=[SCALAR, *[FAST] * n_in, *[ANY] * len(behind), *[SLOW] * n_w],
         out_specs=[FAST] * (n_out + n_a),
         out_shape=[*outputs, *[jax.ShapeDtypeStruct((p.rows, p.columns), BF16) for p in ahead]],
-        scratch_shapes=[pltpu.SemaphoreType.DMA((max(1, n_a),)), *scratch],
-        compiler_params=pltpu.CompilerParams(vmem_limit_bytes=SCOPED),
+        scratch_shapes=[
+            pltpu.SemaphoreType.DMA((max(1, len(moving)),)),
+            *[pltpu.VMEM((p.rows, p.columns), BF16) for p in late],
+            *scratch,
+        ],
+        compiler_params=pltpu.CompilerParams(vmem_limit_bytes=SCOPED + own),
         cost_estimate=pl.CostEstimate(
             flops=flops // COST, bytes_accessed=moved // COST, transcendentals=0
         ),
@@ -116,6 +128,7 @@
         for copy in copies:
             copy.start()
         position = lax.broadcasted_iota(jnp.int32, (heads, cached), 1)
+        owner = lax.broadcasted_iota(jnp.int32, (heads, HD), 0) // groups
 
         def rows_of(ref, b):
             row = ref[b : b + 1, :].astype(F32)
@@ -132,17 +145,13 @@
         weights = []
         for b in range(count):
             q = q_ref[b : b + 1, :].astype(F32).reshape(heads, HD)
-            q_narrow = q.astype(BF16)
-            scores = [
-                lax.dot_general(
-                    q_narrow[g * groups : (g + 1) * groups],
-                    k_ref[b, :, g * HD : (g + 1) * HD],
-                    (((1,), (1,)), ((), ())),
-                    preferred_element_type=F32,
-                )
-                for g in range(KVH)
-            ]
-            scores = jnp.concatenate(scores, axis=0) * score_scale
+            spread = jnp.concatenate(
+                [jnp.where(owner == g, q, 0.0).astype(BF16) for g in range(KVH)], axis=1
+            )
+            scores = lax.dot_general(
+                spread, k_ref[b], (((1,), (1,)), ((), ())), preferred_element_type=F32
+            )
+            scores = scores * score_scale
             own = jnp.sum(q * rows_of(kn_ref, b), axis=-1, keepdims=True) * score_scale
             live = position < length_ref[b]
             scores = jnp.where(live, scores, jnp.float32(-1e30))
@@ -157,13 +166,9 @@
             copy.wait()
         for b in range(count):
             probs, own_prob = weights[b]
+            product = jnp.dot(probs, v_ref[b], preferred_element_type=F32)
             attended = [
-                jnp.dot(
-                    probs[g * groups : (g + 1) * groups],
-                    v_ref[b, :, g * HD : (g + 1) * HD],
-                    preferred_element_type=F32,
-                )
-                for g in range(KVH)
+                product[g * groups : (g + 1) * groups, g * HD : (g + 1) * HD] for g in range(KVH)
             ]
             mixed = jnp.concatenate(attended, axis=0) + own_prob * rows_of(vn_ref, b)
             mixed = mixed + resid_ref[b : b + 1, :].astype(F32).reshape(heads, HD)
@@ -188,17 +193,18 @@
     )(*[pltpu.with_memory_space_constraint(x, pltpu.HBM) for x in (*inputs, gain)])
 
 
-def gate_up(core, x, gates, ups, ahead, behind, places=None):
+def gate_up(core, x, gates, ups, ahead, behind, places=None, late=()):
     depth = gates[0].shape[0]
     pieces = [x] if places is None else x
     rows = x.shape[0] if places is None else sum(p.size for p in pieces) // depth
     half = rows // 2
     m = len(pieces)
     made = [] if places is None else [jax.ShapeDtypeStruct((rows, depth), BF16)]
-    n, tile = len(gates), gates[0].shape[1]
-
-    def kernel(core_ref, in_refs, out_refs, scratch_refs):
-        x_ref, w_refs = in_refs[0], (in_refs[m : n + m], in_refs[n + m :])
+    held, tile = len(gates), gates[0].shape[1]
+    n = held + len(late) // 2
+
+    def kernel(core_ref, in_refs, out_refs, scratch_refs, late_refs=(), copies=()):
+        x_ref, w_refs = in_refs[0], (in_refs[m : held + m], in_refs[held + m :])
         *made_refs, keep_ref, send_ref = out_refs
         for x_ref in made_refs:
             for i in range(m):
@@ -210,7 +216,12 @@
         for j in range(n):
             at = slice(j * tile, (j + 1) * tile)
             for i in range(2):
-                part = jnp.dot(x_ref[...], w_refs[i][j][...], preferred_element_type=F32)
+                if j < held:
+                    w_ref = w_refs[i][j]
+                else:
+                    w_ref = late_refs[2 * (j - held) + i]
+                    copies[2 * (j - held) + i].wait()
+                part = jnp.dot(x_ref[...], w_ref[...], preferred_element_type=F32)
                 keep_ref[i, :, at] = jnp.where(upper, part[:half], part[half:])
                 send_ref[i, :, at] = jnp.where(upper, part[half:], part[:half]).astype(BF16)
 
@@ -228,6 +239,7 @@
         [],
         4 * rows * depth * n * tile,
         behind,
+        late,
     )
 
 
@@ -392,7 +404,8 @@
             [(s * group_rows, group_rows, row_of(s, 1), cut) for s in range(n_far)],
         ]
 
-        plan = [[], gate_up_pieces(chunks[2][1:2]), down_pieces([0])]
+        plan = [[], [], down_pieces([0])]
+        late = gate_up_pieces(chunks[2][1:])
         chips, arrived, mine, theirs = [], [], [], []
 
         def finish(c):
@@ -404,30 +417,24 @@
 
         for c, which in enumerate(chunks):
             behind = [sent] if c else [first_done, done, second_done]
-            if c == 2:
-                bring(chunks[2][2:], [sent])
             (*made, keep, send), pieces = gate_up(
                 core,
                 x if c else x_pieces,
-                [gates[j] for j in which],
-                [ups[j] for j in which],
+                [gates[j] for j in which if j in gates],
+                [ups[j] for j in which if j in ups],
                 plan[c],
                 behind,
                 None if c else places,
+                late if c == 2 else (),
             )
             if c == 0:
                 (x,) = made
-            elif c == 1:
-                take(chunks[2][1:2], pieces)
-            else:
-                downs[0] = pieces[0]
-            if c == 1:
-                send, arrived[-1] = lax.optimization_barrier((send, arrived[-1]))
+            elif c == 2:
+                (downs[0],) = pieces
             chip = keep + narrow_swap(send, 1).astype(F32)
             sent = chip.astype(BF16)
             if c:
                 finish(c - 1)
-            if c > 1:
                 sent, mine[c - 1] = lax.optimization_barrier((sent, mine[c - 1]))
             if c > 1:
                 sent, theirs[0] = lax.optimization_barrier((sent, theirs[0]))

time: 99.8 us -> 98.6 us (0.988)
    pallas_call x11 -> x10, Pallas kernels: 40.7 us -> 40.5 us  [call(): pl.pallas_call(whole, in_specs=[SCALAR, *[FAST] * n_in, *[ANY] * len(behi...]
  transfers between devices with their start and end apart: 31 -> 31, of which waited for: 13 -> 14; matrix products, arithmetic and copies ran while one was open for 1% -> 1% of each run, Pallas kernels for 38% -> 38%
where the time goes in v3:
time: 98.6 us; the launch traced here: 98.4 us
  Pallas kernels  43.5 us (44%)
  starting transfers between devices  31.3 us (32%)
  waiting for transfers between devices  20.5 us (21%)
  other arithmetic  2.61 us (3%)
    pallas_call x10, Pallas kernels, call(): pl.pallas_call(whole, in_specs=[SCALAR, *[FAST] * n_in, *[ANY] * len(behi...  40.5 us
    ppermute x12, starting transfers between devices, far_swap(): return lax.ppermute(x, 'wide', [(i, i ^ slot << 1) for i in range(n_wide)])  16.9 us
    ppermute x15, starting transfers between devices, narrow_swap(): return lax.ppermute(x, 'narrow', [(i, i ^ mask) for i in range(n_narrow)])  9.8 us
    ppermute x15, waiting for transfers between devices, narrow_swap(): return lax.ppermute(x, 'narrow', [(i, i ^ mask) for i in range(n_narrow)])  8.94 us
    ppermute x12, waiting for transfers between devices, far_swap(): return lax.ppermute(x, 'wide', [(i, i ^ slot << 1) for i in range(n_wide)])  8.47 us
    ppermute x4, starting transfers between devices, wide_swap(): return lax.ppermute(x, 'wide', [(i, i ^ 1) for i in range(n_wide)])  4.55 us
    ppermute x4, waiting for transfers between devices, wide_swap(): return lax.ppermute(x, 'wide', [(i, i ^ 1) for i in range(n_wide)])  3.13 us
    pallas_call x1, Pallas kernels, attend(): pl.pallas_call(kernel, in_specs=[SLOW] * (len(inputs) + 1), out_specs=[FA...  3.03 us
  transfers between devices with their start and end apart: 31, of which 14 were waited for; matrix products, arithmetic and copies ran while one was open for 1% of the time, Pallas kernels for 38%

profile of v3, /device:TPU:0, one launch (start us, length us, event | category | flops | bytes accessed | tf_op | source)
XLA Modules:
  0.0 98.4 jit_solution(14832625110219107188)
XLA Ops:
  0.0 3.0 %attend.1 = (f32[4,16384]{1,0:T(4,128)S(1)}, f32[4,128]{1,0:T(4,128)S(1)}, bf16[16384]{0:T(1024)(128)(2,1)S(1)}) custom-call(s32[4]{0:T(128)} %refs_0_.1, bf16[4,16384]{1,0:T(4,128)(2,1)} %refs_1_, bf16[4,192,1024]{2,1,0:T(8,128)(2,1)} %refs_2_.5, bf16[4,1024]{1,0:T(4,128)(2,1)} %refs_3_.4, bf16[4,192,1024]{2,1,0:T(8,128)(2,1)} %refs_4_.1, ...), custom_call_target="tpu_custom_call" | custom-call | tf_op jit(solution)/shard_map/attend/pallas_call | solution.py:181
  3.5 2.4 %collective-permute-start.2 = (bf16[4,4096]{1,0:T(4,128)(2,1)S(1)}, bf16[4,4096]{1,0:T(4,128)(2,1)S(1)}, u32[]{:S(2)}, u32[]{:S(2)}) collective-permute-start(bf16[4,4096]{1,0:T(4,128)(2,1)S(1)} %get-tuple-element.172), channel_id=1, source_target_pairs={{0,3},{1,2},{2,1},{3,0},{4,7},{5,6},{6,5},{7,4},{8,11},{9,10},{10,... | collective-permute-start | bytes 98312 | tf_op jit(solution)/shard_map/ppermute | solution.py:297
  6.6 3.5 %load.4 = (s32[8,128]{1,0:T(8,128)S(1)}, bf16[4096,512]{1,0:T(8,128)(2,1)S(1)}, bf16[4096,512]{1,0:T(8,128)(2,1)S(1)}) custom-call(s32[1]{0:T(128)} %bitcast.refs_0_, bf16[4,16384]{1,0:T(4,128)(2,1)S(1)} %multiply_convert_fusion.refs_1_, bf16[4096,3584]{1,0:T(8,128)(2,1)} %refs_5_.3, bf16[4096,3584]{1,0:T(8,128)(2,1)} %refs_6_.3), custom_call_target="tpu_custom_call" | custom-call | bytes 524288 | tf_op jit(solution)/shard_map/load/pallas_call | solution.py:74
  10.3 1.8 %collective-permute-start.3 = (bf16[16,1536]{1,0:T(8,128)(2,1)S(1)}, bf16[16,1536]{1,0:T(8,128)(2,1)S(1)}, u32[]{:S(2)}, u32[]{:S(2)}) collective-permute-start(bf16[16,1536]{1,0:T(8,128)(2,1)S(1)} %pad_maximum_fusion.5), channel_id=1, source_target_pairs={{0,4},{4,0},{8,12},{12,8},{16,20},{20,16},{24,28},{28,24},{1,5},{5... | collective-permute-start | bytes 147464 | tf_op jit(solution)/shard_map/ppermute | solution.py:300
  12.1 3.7 %collective-permute-start.6 = (bf16[16,2560]{1,0:T(8,128)(2,1)S(1)}, bf16[16,2560]{1,0:T(8,128)(2,1)S(1)}, u32[]{:S(2)}, u32[]{:S(2)}) collective-permute-start(bf16[16,2560]{1,0:T(8,128)(2,1)S(1)} %pad_maximum_fusion.2.refs_5_), channel_id=1, source_target_pairs={{0,24},{4,28},{8,16},{12,20},{16,8},{20,12},{24,0},{28,4},{1,25},{... | collective-permute-start | bytes 245768 | tf_op jit(solution)/shard_map/ppermute | solution.py:303
  16.6 6.0 %load.5 = (s32[8,128]{1,0:T(8,128)S(1)}, bf16[4096,512]{1,0:T(8,128)(2,1)S(1)}, bf16[4096,512]{1,0:T(8,128)(2,1)S(1)}, bf16[4096,512]{1,0:T(8,128)(2,1)S(1)}, bf16[4096,512]{1,0:T(8,128)(2,1)S(1)}) custom-call(s32[1]{0:T(128)} %bitcast.refs_0_, bf16[32,1536]{1,0:T(8,128)(2,1)S(1)} %pad_maximum_fusion.1.refs_1_, bf16[4096,3584]{1,0:T(8,128)(2,1)} %refs_5_.3, ...), custom_call_target="tpu_custom_call" | custom-call | bytes 1048576 | tf_op jit(solution)/shard_map/load/pallas_call | solution.py:74
  23.4 3.4 %collective-permute-start.9 = (bf16[32,1536]{1,0:T(8,128)(2,1)S(1)}, bf16[32,1536]{1,0:T(8,128)(2,1)S(1)}, u32[]{:S(2)}, u32[]{:S(2)}) collective-permute-start(bf16[32,1536]{1,0:T(8,128)(2,1)S(1)} %pad_maximum_fusion.1.refs_1_), channel_id=1, source_target_pairs={{0,24},{4,28},{8,16},{12,20},{16,8},{20,12},{24,0},{28,4},{1,25},{... | collective-permute-start | bytes 294920 | tf_op jit(solution)/shard_map/ppermute | solution.py:303
  27.8 5.9 %load.6 = (s32[8,128]{1,0:T(8,128)S(1)}, bf16[4096,512]{1,0:T(8,128)(2,1)S(1)}, bf16[4096,512]{1,0:T(8,128)(2,1)S(1)}, bf16[4096,512]{1,0:T(8,128)(2,1)S(1)}, bf16[4096,512]{1,0:T(8,128)(2,1)S(1)}) custom-call(s32[1]{0:T(128)} %bitcast.refs_0_, bf16[32,1536]{1,0:T(8,128)(2,1)S(1)} %pad_maximum_fusion.1.refs_1_, bf16[4096,3584]{1,0:T(8,128)(2,1)} %refs_5_.3, ...), custom_call_target="tpu_custom_call" | custom-call | bytes 1048576 | tf_op jit(solution)/shard_map/load/pallas_call | solution.py:74
  34.2 1.3 %gate_up.3 = (bf16[128,4096]{1,0:T(8,128)(2,1)S(1)}, f32[2,64,512]{2,1,0:T(8,128)S(1)}, bf16[2,64,512]{2,1,0:T(8,128)(2,1)S(1)}) custom-call(s32[1]{0:T(128)} %bitcast.refs_0_, bf16[32,1536]{1,0:T(8,128)(2,1)S(1)} %pad_maximum_fusion.1.refs_1_, bf16[32,1536]{1,0:T(8,128)(2,1)S(1)} %collective-permute-done.7.refs_2_, ...), custom_call_target="tpu_custom_call" | custom-call | flops 67108864 | tf_op jit(solution)/shard_map/gate_up/pallas_call | solution.py:74
  35.6 1.3 %collective-permute-done.11 = bf16[2,64,512]{2,1,0:T(8,128)(2,1)S(1)} collective-permute-done((bf16[2,64,512]{2,1,0:T(8,128)(2,1)S(1)}, bf16[2,64,512]{2,1,0:T(8,128)(2,1)S(1)}, u32[]{:S(2)}, u32[]{:S(2)}) %collective-permute-start.11) | collective-permute-done | bytes 131104 | tf_op jit(solution)/shard_map/ppermute | solution.py:297
  37.0 1.6 %collective-permute-start.13 = (bf16[2,64,512]{2,1,0:T(8,128)(2,1)S(1)}, bf16[2,64,512]{2,1,0:T(8,128)(2,1)S(1)}, u32[]{:S(2)}, u32[]{:S(2)}) collective-permute-start(bf16[2,64,512]{2,1,0:T(8,128)(2,1)S(1)} %fusion.6.refs_8_), channel_id=1, source_target_pairs={{0,2},{1,3},{2,0},{3,1},{4,6},{5,7},{6,4},{7,5},{8,10},{9,11},{10,... | collective-permute-start | bytes 393224 | tf_op jit(solution)/shard_map/ppermute | solution.py:297
  38.6 3.5 %gate_up.4 = (f32[2,64,1536]{2,1,0:T(8,128)S(1)}, bf16[2,64,1536]{2,1,0:T(8,128)(2,1)S(1)}) custom-call(s32[1]{0:T(128)} %bitcast.refs_0_, bf16[128,4096]{1,0:T(8,128)(2,1)S(1)} %get-tuple-element.114.refs_1_, bf16[4096,512]{1,0:T(8,128)(2,1)S(1)} %get-tuple-element.117.refs_2_, bf16[4096,512]{1,0:T(8,128)(2,1)S(1)} %get-tuple-element.118.refs_3_, ...), custom_call_target="tpu_custom_call" | custom-call | flops 201326592 | tf_op jit(solution)/shard_map/gate_up/pallas_call | solution.py:74
  44.5 8.3 %gate_up.5 = (f32[2,64,1536]{2,1,0:T(8,128)S(1)}, bf16[2,64,1536]{2,1,0:T(8,128)(2,1)S(1)}, bf16[512,4096]{1,0:T(8,128)(2,1)S(1)}) custom-call(s32[1]{0:T(128)} %bitcast.refs_0_, bf16[128,4096]{1,0:T(8,128)(2,1)S(1)} %get-tuple-element.114.refs_1_, bf16[4096,512]{1,0:T(8,128)(2,1)S(1)} %get-tuple-element.115.refs_2_, ...), custom_call_target="tpu_custom_call" | custom-call | flops 201326592 | bytes 1310720 | tf_op jit(solution)/shard_map/gate_up/pallas_call | solution.py:74
  53.3 1.8 %collective-permute-done.15 = bf16[2,64,1536]{2,1,0:T(8,128)(2,1)S(1)} collective-permute-done((bf16[2,64,1536]{2,1,0:T(8,128)(2,1)S(1)}, bf16[2,64,1536]{2,1,0:T(8,128)(2,1)S(1)}, u32[]{:S(2)}, u32[]{:S(2)}) %collective-permute-start.15) | collective-permute-done | bytes 393248 | tf_op jit(solution)/shard_map/ppermute | solution.py:297
  56.6 5.2 %load.7 = (s32[8,128]{1,0:T(8,128)}, bf16[1536,4096]{1,0:T(8,128)(2,1)S(1)}) custom-call(s32[1]{0:T(128)} %bitcast.refs_0_, bf16[2,64,1536]{2,1,0:T(8,128)(2,1)S(1)} %fusion.1.refs_1_, bf16[3584,4096]{1,0:T(8,128)(2,1)} %refs_7_.5), custom_call_target="tpu_custom_call" | custom-call | bytes 786432 | tf_op jit(solution)/shard_map/load/pallas_call | solution.py:74
  61.8 4.6 %down.3 = (f32[128,4096]{1,0:T(8,128)S(1)}, bf16[1536,4096]{1,0:T(8,128)(2,1)S(1)}) custom-call(s32[1]{0:T(128)} %bitcast.refs_0_, bf16[64,512]{1,0:T(8,128)(2,1)S(1)} %fusion.11.refs_1_, bf16[64,1536]{1,0:T(8,128)(2,1)S(1)} %fusion.5.refs_2_, bf16[64,512]{1,0:T(8,128)(2,1)S(1)} %collective-permute-done.16.refs_3_, ...), custom_call_target="tpu_custom_call" | custom-call | flops 134217728 | bytes 786432 | tf_op jit(solution)/shard_map/down/pallas_call | solution.py:74
  69.5 1.6 %collective-permute-start.20 = (bf16[64,2560]{1,0:T(8,128)(2,1)S(1)}, bf16[64,2560]{1,0:T(8,128)(2,1)S(1)}, u32[]{:S(2)}, u32[]{:S(2)}) collective-permute-start(bf16[64,2560]{1,0:T(8,128)(2,1)S(1)} %get-tuple-element.142.refs_5_), channel_id=1, source_target_pairs={{0,4},{4,0},{8,12},{12,8},{16,20},{20,16},{24,28},{28,24},{1,5},{5... | collective-permute-start | bytes 983048 | tf_op jit(solution)/shard_map/ppermute | solution.py:300
  72.7 2.9 %collective-permute-start.22 = (bf16[32,1536]{1,0:T(8,128)(2,1)S(1)}, bf16[32,1536]{1,0:T(8,128)(2,1)S(1)}, u32[]{:S(2)}, u32[]{:S(2)}) collective-permute-start(bf16[32,1536]{1,0:T(8,128)(2,1)S(1)} %get-tuple-element.144), channel_id=1, source_target_pairs={{0,16},{4,20},{8,24},{12,28},{16,0},{20,4},{24,8},{28,12},{1,17},{... | collective-permute-start | bytes 294920 | tf_op jit(solution)/shard_map/ppermute | solution.py:303
  76.5 3.1 %collective-permute-done.20 = bf16[64,2560]{1,0:T(8,128)(2,1)S(1)} collective-permute-done((bf16[64,2560]{1,0:T(8,128)(2,1)S(1)}, bf16[64,2560]{1,0:T(8,128)(2,1)S(1)}, u32[]{:S(2)}, u32[]{:S(2)}) %collective-permute-start.20) | collective-permute-done | bytes 327712 | tf_op jit(solution)/shard_map/ppermute | solution.py:300
  80.4 2.4 %collective-permute-start.26 = (bf16[16,2560]{1,0:T(8,128)(2,1)S(1)}, bf16[16,2560]{1,0:T(8,128)(2,1)S(1)}, u32[]{:S(2)}, u32[]{:S(2)}) collective-permute-start(bf16[16,2560]{1,0:T(8,128)(2,1)S(1)} %get-tuple-element.160), channel_id=1, source_target_pairs={{0,24},{4,28},{8,16},{12,20},{16,8},{20,12},{24,0},{28,4},{1,25},{... | collective-permute-start | bytes 245768 | tf_op jit(solution)/shard_map/ppermute | solution.py:303
  83.5 2.1 %collective-permute-done.24 = bf16[16,2560]{1,0:T(8,128)(2,1)S(1)} collective-permute-done((bf16[16,2560]{1,0:T(8,128)(2,1)S(1)}, bf16[16,2560]{1,0:T(8,128)(2,1)S(1)}, u32[]{:S(2)}, u32[]{:S(2)}) %collective-permute-start.24) | collective-permute-done | bytes 81952 | tf_op jit(solution)/shard_map/ppermute | solution.py:303
  86.2 1.3 %collective-permute-done.26 = bf16[16,2560]{1,0:T(8,128)(2,1)S(1)} collective-permute-done((bf16[16,2560]{1,0:T(8,128)(2,1)S(1)}, bf16[16,2560]{1,0:T(8,128)(2,1)S(1)}, u32[]{:S(2)}, u32[]{:S(2)}) %collective-permute-start.26) | collective-permute-done | bytes 81952 | tf_op jit(solution)/shard_map/ppermute | solution.py:303
  87.6 4.2 %collective-permute-done.25 = bf16[16,2560]{1,0:T(8,128)(2,1)S(1)} collective-permute-done((bf16[16,2560]{1,0:T(8,128)(2,1)S(1)}, bf16[16,2560]{1,0:T(8,128)(2,1)S(1)}, u32[]{:S(2)}, u32[]{:S(2)}) %collective-permute-start.25) | collective-permute-done | bytes 81952 | tf_op jit(solution)/shard_map/ppermute | solution.py:303
  95.7 1.8 %collective-permute-done.29 = bf16[4,4096]{1,0:T(4,128)(2,1)S(1)} collective-permute-done((bf16[4,4096]{1,0:T(4,128)(2,1)S(1)}, bf16[4,4096]{1,0:T(4,128)(2,1)S(1)}, u32[]{:S(2)}, u32[]{:S(2)}) %collective-permute-start.29) | collective-permute-done | bytes 32800 | tf_op jit(solution)/shard_map/ppermute | solution.py:297
  (77 shorter events, 21.1 us)
Async XLA Ops:
  3.5 6.6 %collective-permute-start.2 = (bf16[4,4096]{1,0:T(4,128)(2,1)S(1)}, bf16[4,4096]{1,0:T(4,128)(2,1)S(1)}, u32[]{:S(2)}, u32[]{:S(2)}) collective-permute-start(bf16[4,4096]{1,0:T(4,128)(2,1)S(1)} %get-tuple-element.172), channel_id=1, source_target_pairs={{0,3},{1,2},{2,1},{3,0},{4,7},{5,6},{6,5},{7,4},{8,11},{9,10},{10,... | collective-permute-start | bytes 98312 | tf_op jit(solution)/shard_map/ppermute | solution.py:297
  5.9 4.2 %collective-permute-start.1 = (bf16[4,4096]{1,0:T(4,128)(2,1)S(1)}, bf16[4,4096]{1,0:T(4,128)(2,1)S(1)}, u32[]{:S(2)}, u32[]{:S(2)}) collective-permute-start(bf16[4,4096]{1,0:T(4,128)(2,1)S(1)} %get-tuple-element.173), channel_id=1, source_target_pairs={{0,2},{1,3},{2,0},{3,1},{4,6},{5,7},{6,4},{7,5},{8,10},{9,11},{10,... | collective-permute-start | bytes 98312 | tf_op jit(solution)/shard_map/ppermute | solution.py:297
  10.3 6.3 %collective-permute-start.3 = (bf16[16,1536]{1,0:T(8,128)(2,1)S(1)}, bf16[16,1536]{1,0:T(8,128)(2,1)S(1)}, u32[]{:S(2)}, u32[]{:S(2)}) collective-permute-start(bf16[16,1536]{1,0:T(8,128)(2,1)S(1)} %pad_maximum_fusion.5), channel_id=1, source_target_pairs={{0,4},{4,0},{8,12},{12,8},{16,20},{20,16},{24,28},{28,24},{1,5},{5... | collective-permute-start | bytes 147464 | tf_op jit(solution)/shard_map/ppermute | solution.py:300
  12.1 10.4 %collective-permute-start.6 = (bf16[16,2560]{1,0:T(8,128)(2,1)S(1)}, bf16[16,2560]{1,0:T(8,128)(2,1)S(1)}, u32[]{:S(2)}, u32[]{:S(2)}) collective-permute-start(bf16[16,2560]{1,0:T(8,128)(2,1)S(1)} %pad_maximum_fusion.2.refs_5_), channel_id=1, source_target_pairs={{0,24},{4,28},{8,16},{12,20},{16,8},{20,12},{24,0},{28,4},{1,25},{... | collective-permute-start | bytes 245768 | tf_op jit(solution)/shard_map/ppermute | solution.py:303
  15.8 7.0 %collective-permute-start.5 = (bf16[16,2560]{1,0:T(8,128)(2,1)S(1)}, bf16[16,2560]{1,0:T(8,128)(2,1)S(1)}, u32[]{:S(2)}, u32[]{:S(2)}) collective-permute-start(bf16[16,2560]{1,0:T(8,128)(2,1)S(1)} %pad_maximum_fusion.2.refs_5_), channel_id=1, source_target_pairs={{0,16},{4,20},{8,24},{12,28},{16,0},{20,4},{24,8},{28,12},{1,17},{... | collective-permute-start | bytes 245768 | tf_op jit(solution)/shard_map/ppermute | solution.py:303
  15.8 7.0 %collective-permute-start.4 = (bf16[16,2560]{1,0:T(8,128)(2,1)S(1)}, bf16[16,2560]{1,0:T(8,128)(2,1)S(1)}, u32[]{:S(2)}, u32[]{:S(2)}) collective-permute-start(bf16[16,2560]{1,0:T(8,128)(2,1)S(1)} %pad_maximum_fusion.2.refs_5_), channel_id=1, source_target_pairs={{0,8},{4,12},{8,0},{12,4},{16,24},{20,28},{24,16},{28,20},{1,9},{5... | collective-permute-start | bytes 245768 | tf_op jit(solution)/shard_map/ppermute | solution.py:303
  22.8 11.4 %collective-permute-start.10 = (bf16[64,2560]{1,0:T(8,128)(2,1)S(1)}, bf16[64,2560]{1,0:T(8,128)(2,1)S(1)}, u32[]{:S(2)}, u32[]{:S(2)}) collective-permute-start(bf16[64,2560]{1,0:T(8,128)(2,1)S(1)} %pad_maximum_fusion), channel_id=1, source_target_pairs={{0,4},{4,0},{8,12},{12,8},{16,20},{20,16},{24,28},{28,24},{1,5},{5... | collective-permute-start | bytes 983048 | tf_op jit(solution)/shard_map/ppermute | solution.py:300
  23.4 10.3 %collective-permute-start.9 = (bf16[32,1536]{1,0:T(8,128)(2,1)S(1)}, bf16[32,1536]{1,0:T(8,128)(2,1)S(1)}, u32[]{:S(2)}, u32[]{:S(2)}) collective-permute-start(bf16[32,1536]{1,0:T(8,128)(2,1)S(1)} %pad_maximum_fusion.1.refs_1_), channel_id=1, source_target_pairs={{0,24},{4,28},{8,16},{12,20},{16,8},{20,12},{24,0},{28,4},{1,25},{... | collective-permute-start | bytes 294920 | tf_op jit(solution)/shard_map/ppermute | solution.py:303
  26.8 7.3 %collective-permute-start.8 = (bf16[32,1536]{1,0:T(8,128)(2,1)S(1)}, bf16[32,1536]{1,0:T(8,128)(2,1)S(1)}, u32[]{:S(2)}, u32[]{:S(2)}) collective-permute-start(bf16[32,1536]{1,0:T(8,128)(2,1)S(1)} %pad_maximum_fusion.1.refs_1_), channel_id=1, source_target_pairs={{0,16},{4,20},{8,24},{12,28},{16,0},{20,4},{24,8},{28,12},{1,17},{... | collective-permute-start | bytes 294920 | tf_op jit(solution)/shard_map/ppermute | solution.py:303
  26.8 7.3 %collective-permute-start.7 = (bf16[32,1536]{1,0:T(8,128)(2,1)S(1)}, bf16[32,1536]{1,0:T(8,128)(2,1)S(1)}, u32[]{:S(2)}, u32[]{:S(2)}) collective-permute-start(bf16[32,1536]{1,0:T(8,128)(2,1)S(1)} %pad_maximum_fusion.1.refs_1_), channel_id=1, source_target_pairs={{0,8},{4,12},{8,0},{12,4},{16,24},{20,28},{24,16},{28,20},{1,9},{5... | collective-permute-start | bytes 294920 | tf_op jit(solution)/shard_map/ppermute | solution.py:303
  37.0 5.6 %collective-permute-start.13 = (bf16[2,64,512]{2,1,0:T(8,128)(2,1)S(1)}, bf16[2,64,512]{2,1,0:T(8,128)(2,1)S(1)}, u32[]{:S(2)}, u32[]{:S(2)}) collective-permute-start(bf16[2,64,512]{2,1,0:T(8,128)(2,1)S(1)} %fusion.6.refs_8_), channel_id=1, source_target_pairs={{0,2},{1,3},{2,0},{3,1},{4,6},{5,7},{6,4},{7,5},{8,10},{9,11},{10,... | collective-permute-start | bytes 393224 | tf_op jit(solution)/shard_map/ppermute | solution.py:297
  43.9 11.2 %collective-permute-start.15 = (bf16[2,64,1536]{2,1,0:T(8,128)(2,1)S(1)}, bf16[2,64,1536]{2,1,0:T(8,128)(2,1)S(1)}, u32[]{:S(2)}, u32[]{:S(2)}) collective-permute-start(bf16[2,64,1536]{2,1,0:T(8,128)(2,1)S(1)} %fusion.refs_4_), channel_id=1, source_target_pairs={{0,2},{1,3},{2,0},{3,1},{4,6},{5,7},{6,4},{7,5},{8,10},{9,11},{10,... | collective-permute-start | bytes 1179656 | tf_op jit(solution)/shard_map/ppermute | solution.py:297
  44.5 11.0 %collective-permute-start.16 = (bf16[64,512]{1,0:T(8,128)(2,1)S(1)}, bf16[64,512]{1,0:T(8,128)(2,1)S(1)}, u32[]{:S(2)}, u32[]{:S(2)}) collective-permute-start(bf16[64,512]{1,0:T(8,128)(2,1)S(1)} %fusion.11.refs_1_), channel_id=1, source_target_pairs={{0,1},{1,0},{2,3},{3,2},{4,5},{5,4},{6,7},{7,6},{8,9},{9,8},{10,11... | collective-permute-start | bytes 196616 | tf_op jit(solution)/shard_map/ppermute | solution.py:297
  55.5 10.9 %collective-permute-start.18 = (bf16[2,64,1536]{2,1,0:T(8,128)(2,1)S(1)}, bf16[2,64,1536]{2,1,0:T(8,128)(2,1)S(1)}, u32[]{:S(2)}, u32[]{:S(2)}) collective-permute-start(bf16[2,64,1536]{2,1,0:T(8,128)(2,1)S(1)} %fusion.1.refs_1_), channel_id=1, source_target_pairs={{0,2},{1,3},{2,0},{3,1},{4,6},{5,7},{6,4},{7,5},{8,10},{9,11},{10,... | collective-permute-start | bytes 1179656 | tf_op jit(solution)/shard_map/ppermute | solution.py:297
  56.5 5.3 %collective-permute-start.17 = (bf16[64,1536]{1,0:T(8,128)(2,1)S(1)}, bf16[64,1536]{1,0:T(8,128)(2,1)S(1)}, u32[]{:S(2)}, u32[]{:S(2)}) collective-permute-start(bf16[64,1536]{1,0:T(8,128)(2,1)S(1)} %fusion.5.refs_2_), channel_id=1, source_target_pairs={{0,1},{1,0},{2,3},{3,2},{4,5},{5,4},{6,7},{7,6},{8,9},{9,8},{10,11... | collective-permute-start | bytes 589832 | tf_op jit(solution)/shard_map/ppermute | solution.py:297
  69.5 10.1 %collective-permute-start.20 = (bf16[64,2560]{1,0:T(8,128)(2,1)S(1)}, bf16[64,2560]{1,0:T(8,128)(2,1)S(1)}, u32[]{:S(2)}, u32[]{:S(2)}) collective-permute-start(bf16[64,2560]{1,0:T(8,128)(2,1)S(1)} %get-tuple-element.142.refs_5_), channel_id=1, source_target_pairs={{0,4},{4,0},{8,12},{12,8},{16,20},{20,16},{24,28},{28,24},{1,5},{5... | collective-permute-start | bytes 983048 | tf_op jit(solution)/shard_map/ppermute | solution.py:300
  72.0 10.8 %collective-permute-start.21 = (bf16[32,1536]{1,0:T(8,128)(2,1)S(1)}, bf16[32,1536]{1,0:T(8,128)(2,1)S(1)}, u32[]{:S(2)}, u32[]{:S(2)}) collective-permute-start(bf16[32,1536]{1,0:T(8,128)(2,1)S(1)} %get-tuple-element.143), channel_id=1, source_target_pairs={{0,8},{4,12},{8,0},{12,4},{16,24},{20,28},{24,16},{28,20},{1,9},{5... | collective-permute-start | bytes 294920 | tf_op jit(solution)/shard_map/ppermute | solution.py:303
  72.7 10.8 %collective-permute-start.22 = (bf16[32,1536]{1,0:T(8,128)(2,1)S(1)}, bf16[32,1536]{1,0:T(8,128)(2,1)S(1)}, u32[]{:S(2)}, u32[]{:S(2)}) collective-permute-start(bf16[32,1536]{1,0:T(8,128)(2,1)S(1)} %get-tuple-element.144), channel_id=1, source_target_pairs={{0,16},{4,20},{8,24},{12,28},{16,0},{20,4},{24,8},{28,12},{1,17},{... | collective-permute-start | bytes 294920 | tf_op jit(solution)/shard_map/ppermute | solution.py:303
  75.6 7.9 %collective-permute-start.23 = (bf16[32,1536]{1,0:T(8,128)(2,1)S(1)}, bf16[32,1536]{1,0:T(8,128)(2,1)S(1)}, u32[]{:S(2)}, u32[]{:S(2)}) collective-permute-start(bf16[32,1536]{1,0:T(8,128)(2,1)S(1)} %get-tuple-element.145), channel_id=1, source_target_pairs={{0,24},{4,28},{8,16},{12,20},{16,8},{20,12},{24,0},{28,4},{1,25},{... | collective-permute-start | bytes 294920 | tf_op jit(solution)/shard_map/ppermute | solution.py:303
  79.7 5.9 %collective-permute-start.24 = (bf16[16,2560]{1,0:T(8,128)(2,1)S(1)}, bf16[16,2560]{1,0:T(8,128)(2,1)S(1)}, u32[]{:S(2)}, u32[]{:S(2)}) collective-permute-start(bf16[16,2560]{1,0:T(8,128)(2,1)S(1)} %get-tuple-element.159), channel_id=1, source_target_pairs={{0,8},{4,12},{8,0},{12,4},{16,24},{20,28},{24,16},{28,20},{1,9},{5... | collective-permute-start | bytes 245768 | tf_op jit(solution)/shard_map/ppermute | solution.py:303
  80.4 7.2 %collective-permute-start.26 = (bf16[16,2560]{1,0:T(8,128)(2,1)S(1)}, bf16[16,2560]{1,0:T(8,128)(2,1)S(1)}, u32[]{:S(2)}, u32[]{:S(2)}) collective-permute-start(bf16[16,2560]{1,0:T(8,128)(2,1)S(1)} %get-tuple-element.160), channel_id=1, source_target_pairs={{0,24},{4,28},{8,16},{12,20},{16,8},{20,12},{24,0},{28,4},{1,25},{... | collective-permute-start | bytes 245768 | tf_op jit(solution)/shard_map/ppermute | solution.py:303
  82.8 8.9 %collective-permute-start.25 = (bf16[16,2560]{1,0:T(8,128)(2,1)S(1)}, bf16[16,2560]{1,0:T(8,128)(2,1)S(1)}, u32[]{:S(2)}, u32[]{:S(2)}) collective-permute-start(bf16[16,2560]{1,0:T(8,128)(2,1)S(1)} %get-tuple-element.161), channel_id=1, source_target_pairs={{0,16},{4,20},{8,24},{12,28},{16,0},{20,4},{24,8},{28,12},{1,17},{... | collective-permute-start | bytes 245768 | tf_op jit(solution)/shard_map/ppermute | solution.py:303
  85.7 6.2 %collective-permute-start.27 = (bf16[16,1536]{1,0:T(8,128)(2,1)S(1)}, bf16[16,1536]{1,0:T(8,128)(2,1)S(1)}, u32[]{:S(2)}, u32[]{:S(2)}) collective-permute-start(bf16[16,1536]{1,0:T(8,128)(2,1)S(1)} %slice.109), channel_id=1, source_target_pairs={{0,4},{4,0},{8,12},{12,8},{16,20},{20,16},{24,28},{28,24},{1,5},{5... | collective-permute-start | bytes 147464 | tf_op jit(solution)/shard_map/ppermute | solution.py:300
  93.6 3.9 %collective-permute-start.29 = (bf16[4,4096]{1,0:T(4,128)(2,1)S(1)}, bf16[4,4096]{1,0:T(4,128)(2,1)S(1)}, u32[]{:S(2)}, u32[]{:S(2)}) collective-permute-start(bf16[4,4096]{1,0:T(4,128)(2,1)S(1)} %get-tuple-element.167), channel_id=1, source_target_pairs={{0,2},{1,3},{2,0},{3,1},{4,6},{5,7},{6,4},{7,5},{8,10},{9,11},{10,... | collective-permute-start | bytes 98312 | tf_op jit(solution)/shard_map/ppermute | solution.py:297
  (7 other events, 16.5 us)

commit v4 on v3

--- a/solution.py
+++ b/solution.py
@@ -412,7 +412,13 @@
             total = chips[c]
             for part in arrived[c]:
                 total = total + part.astype(F32)
-            hidden = (jax.nn.silu(total[0]) * total[1]).astype(BF16)
+            gate, up = total[0], total[1]
+            if c == len(chunks) - 1:
+                gate, up = chips[c][0], chips[c][1]
+                for part in arrived[c]:
+                    gate = gate + part[0].astype(F32)
+                    up = up + part[1].astype(F32)
+            hidden = (jax.nn.silu(gate) * up).astype(BF16)
             mine.append(hidden)
 
         for c, which in enumerate(chunks):

time: 98.6 us -> 98.6 us (level)
  no operation moved by 1% of the time
where the time goes in v4:
time: 98.6 us; the launch traced here: 98.4 us
  Pallas kernels  43.5 us (44%)
  starting transfers between devices  31.3 us (32%)
  waiting for transfers between devices  20.5 us (21%)
  other arithmetic  2.58 us (3%)
    pallas_call x10, Pallas kernels, call(): pl.pallas_call(whole, in_specs=[SCALAR, *[FAST] * n_in, *[ANY] * len(behi...  40.4 us
    ppermute x12, starting transfers between devices, far_swap(): return lax.ppermute(x, 'wide', [(i, i ^ slot << 1) for i in range(n_wide)])  16.9 us
    ppermute x15, starting transfers between devices, narrow_swap(): return lax.ppermute(x, 'narrow', [(i, i ^ mask) for i in range(n_narrow)])  9.8 us
    ppermute x15, waiting for transfers between devices, narrow_swap(): return lax.ppermute(x, 'narrow', [(i, i ^ mask) for i in range(n_narrow)])  8.94 us
    ppermute x12, waiting for transfers between devices, far_swap(): return lax.ppermute(x, 'wide', [(i, i ^ slot << 1) for i in range(n_wide)])  8.46 us
    ppermute x4, starting transfers between devices, wide_swap(): return lax.ppermute(x, 'wide', [(i, i ^ 1) for i in range(n_wide)])  4.56 us
    ppermute x4, waiting for transfers between devices, wide_swap(): return lax.ppermute(x, 'wide', [(i, i ^ 1) for i in range(n_wide)])  3.13 us
    pallas_call x1, Pallas kernels, attend(): pl.pallas_call(kernel, in_specs=[SLOW] * (len(inputs) + 1), out_specs=[FA...  3.03 us
  transfers between devices with their start and end apart: 31, of which 14 were waited for; matrix products, arithmetic and copies ran while one was open for 1% of the time, Pallas kernels for 38%

profile of v4, /device:TPU:0, one launch (start us, length us, event | category | flops | bytes accessed | tf_op | source)
XLA Modules:
  0.0 98.4 jit_solution(8749950506419605132)
XLA Ops:
  0.0 3.0 %attend.1 = (f32[4,16384]{1,0:T(4,128)S(1)}, f32[4,128]{1,0:T(4,128)S(1)}, bf16[16384]{0:T(1024)(128)(2,1)S(1)}) custom-call(s32[4]{0:T(128)} %refs_0_.1, bf16[4,16384]{1,0:T(4,128)(2,1)} %refs_1_, bf16[4,192,1024]{2,1,0:T(8,128)(2,1)} %refs_2_.5, bf16[4,1024]{1,0:T(4,128)(2,1)} %refs_3_.4, bf16[4,192,1024]{2,1,0:T(8,128)(2,1)} %refs_4_.1, ...), custom_call_target="tpu_custom_call" | custom-call | tf_op jit(solution)/shard_map/attend/pallas_call | solution.py:181
  3.5 2.4 %collective-permute-start.2 = (bf16[4,4096]{1,0:T(4,128)(2,1)S(1)}, bf16[4,4096]{1,0:T(4,128)(2,1)S(1)}, u32[]{:S(2)}, u32[]{:S(2)}) collective-permute-start(bf16[4,4096]{1,0:T(4,128)(2,1)S(1)} %get-tuple-element.174), channel_id=1, source_target_pairs={{0,3},{1,2},{2,1},{3,0},{4,7},{5,6},{6,5},{7,4},{8,11},{9,10},{10,... | collective-permute-start | bytes 98312 | tf_op jit(solution)/shard_map/ppermute | solution.py:297
  6.6 3.5 %load.4 = (s32[8,128]{1,0:T(8,128)S(1)}, bf16[4096,512]{1,0:T(8,128)(2,1)S(1)}, bf16[4096,512]{1,0:T(8,128)(2,1)S(1)}) custom-call(s32[1]{0:T(128)} %bitcast.refs_0_, bf16[4,16384]{1,0:T(4,128)(2,1)S(1)} %multiply_convert_fusion.refs_1_, bf16[4096,3584]{1,0:T(8,128)(2,1)} %refs_5_.3, bf16[4096,3584]{1,0:T(8,128)(2,1)} %refs_6_.3), custom_call_target="tpu_custom_call" | custom-call | bytes 524288 | tf_op jit(solution)/shard_map/load/pallas_call | solution.py:74
  10.3 1.8 %collective-permute-start.3 = (bf16[16,1536]{1,0:T(8,128)(2,1)S(1)}, bf16[16,1536]{1,0:T(8,128)(2,1)S(1)}, u32[]{:S(2)}, u32[]{:S(2)}) collective-permute-start(bf16[16,1536]{1,0:T(8,128)(2,1)S(1)} %pad_maximum_fusion.5), channel_id=1, source_target_pairs={{0,4},{4,0},{8,12},{12,8},{16,20},{20,16},{24,28},{28,24},{1,5},{5... | collective-permute-start | bytes 147464 | tf_op jit(solution)/shard_map/ppermute | solution.py:300
  12.1 3.7 %collective-permute-start.6 = (bf16[16,2560]{1,0:T(8,128)(2,1)S(1)}, bf16[16,2560]{1,0:T(8,128)(2,1)S(1)}, u32[]{:S(2)}, u32[]{:S(2)}) collective-permute-start(bf16[16,2560]{1,0:T(8,128)(2,1)S(1)} %pad_maximum_fusion.2.refs_5_), channel_id=1, source_target_pairs={{0,24},{4,28},{8,16},{12,20},{16,8},{20,12},{24,0},{28,4},{1,25},{... | collective-permute-start | bytes 245768 | tf_op jit(solution)/shard_map/ppermute | solution.py:303
  16.6 6.0 %load.5 = (s32[8,128]{1,0:T(8,128)S(1)}, bf16[4096,512]{1,0:T(8,128)(2,1)S(1)}, bf16[4096,512]{1,0:T(8,128)(2,1)S(1)}, bf16[4096,512]{1,0:T(8,128)(2,1)S(1)}, bf16[4096,512]{1,0:T(8,128)(2,1)S(1)}) custom-call(s32[1]{0:T(128)} %bitcast.refs_0_, bf16[32,1536]{1,0:T(8,128)(2,1)S(1)} %pad_maximum_fusion.1.refs_1_, bf16[4096,3584]{1,0:T(8,128)(2,1)} %refs_5_.3, ...), custom_call_target="tpu_custom_call" | custom-call | bytes 1048576 | tf_op jit(solution)/shard_map/load/pallas_call | solution.py:74
  23.4 3.4 %collective-permute-start.9 = (bf16[32,1536]{1,0:T(8,128)(2,1)S(1)}, bf16[32,1536]{1,0:T(8,128)(2,1)S(1)}, u32[]{:S(2)}, u32[]{:S(2)}) collective-permute-start(bf16[32,1536]{1,0:T(8,128)(2,1)S(1)} %pad_maximum_fusion.1.refs_1_), channel_id=1, source_target_pairs={{0,24},{4,28},{8,16},{12,20},{16,8},{20,12},{24,0},{28,4},{1,25},{... | collective-permute-start | bytes 294920 | tf_op jit(solution)/shard_map/ppermute | solution.py:303
  27.8 5.9 %load.6 = (s32[8,128]{1,0:T(8,128)S(1)}, bf16[4096,512]{1,0:T(8,128)(2,1)S(1)}, bf16[4096,512]{1,0:T(8,128)(2,1)S(1)}, bf16[4096,512]{1,0:T(8,128)(2,1)S(1)}, bf16[4096,512]{1,0:T(8,128)(2,1)S(1)}) custom-call(s32[1]{0:T(128)} %bitcast.refs_0_, bf16[32,1536]{1,0:T(8,128)(2,1)S(1)} %pad_maximum_fusion.1.refs_1_, bf16[4096,3584]{1,0:T(8,128)(2,1)} %refs_5_.3, ...), custom_call_target="tpu_custom_call" | custom-call | bytes 1048576 | tf_op jit(solution)/shard_map/load/pallas_call | solution.py:74
  34.2 1.3 %gate_up.3 = (bf16[128,4096]{1,0:T(8,128)(2,1)S(1)}, f32[2,64,512]{2,1,0:T(8,128)S(1)}, bf16[2,64,512]{2,1,0:T(8,128)(2,1)S(1)}) custom-call(s32[1]{0:T(128)} %bitcast.refs_0_, bf16[32,1536]{1,0:T(8,128)(2,1)S(1)} %pad_maximum_fusion.1.refs_1_, bf16[32,1536]{1,0:T(8,128)(2,1)S(1)} %collective-permute-done.7.refs_2_, ...), custom_call_target="tpu_custom_call" | custom-call | flops 67108864 | tf_op jit(solution)/shard_map/gate_up/pallas_call | solution.py:74
  35.6 1.3 %collective-permute-done.11 = bf16[2,64,512]{2,1,0:T(8,128)(2,1)S(1)} collective-permute-done((bf16[2,64,512]{2,1,0:T(8,128)(2,1)S(1)}, bf16[2,64,512]{2,1,0:T(8,128)(2,1)S(1)}, u32[]{:S(2)}, u32[]{:S(2)}) %collective-permute-start.11) | collective-permute-done | bytes 131104 | tf_op jit(solution)/shard_map/ppermute | solution.py:297
  37.0 1.6 %collective-permute-start.13 = (bf16[2,64,512]{2,1,0:T(8,128)(2,1)S(1)}, bf16[2,64,512]{2,1,0:T(8,128)(2,1)S(1)}, u32[]{:S(2)}, u32[]{:S(2)}) collective-permute-start(bf16[2,64,512]{2,1,0:T(8,128)(2,1)S(1)} %fusion.7.refs_8_), channel_id=1, source_target_pairs={{0,2},{1,3},{2,0},{3,1},{4,6},{5,7},{6,4},{7,5},{8,10},{9,11},{10,... | collective-permute-start | bytes 393224 | tf_op jit(solution)/shard_map/ppermute | solution.py:297
  38.6 3.5 %gate_up.4 = (f32[2,64,1536]{2,1,0:T(8,128)S(1)}, bf16[2,64,1536]{2,1,0:T(8,128)(2,1)S(1)}) custom-call(s32[1]{0:T(128)} %bitcast.refs_0_, bf16[128,4096]{1,0:T(8,128)(2,1)S(1)} %get-tuple-element.114.refs_1_, bf16[4096,512]{1,0:T(8,128)(2,1)S(1)} %get-tuple-element.117.refs_2_, bf16[4096,512]{1,0:T(8,128)(2,1)S(1)} %get-tuple-element.118.refs_3_, ...), custom_call_target="tpu_custom_call" | custom-call | flops 201326592 | tf_op jit(solution)/shard_map/gate_up/pallas_call | solution.py:74
  44.5 8.3 %gate_up.5 = (f32[2,64,1536]{2,1,0:T(8,128)S(1)}, bf16[2,64,1536]{2,1,0:T(8,128)(2,1)S(1)}, bf16[512,4096]{1,0:T(8,128)(2,1)S(1)}) custom-call(s32[1]{0:T(128)} %bitcast.refs_0_, bf16[128,4096]{1,0:T(8,128)(2,1)S(1)} %get-tuple-element.114.refs_1_, bf16[4096,512]{1,0:T(8,128)(2,1)S(1)} %get-tuple-element.115.refs_2_, ...), custom_call_target="tpu_custom_call" | custom-call | flops 201326592 | bytes 1310720 | tf_op jit(solution)/shard_map/gate_up/pallas_call | solution.py:74
  53.3 1.8 %collective-permute-done.15 = bf16[2,64,1536]{2,1,0:T(8,128)(2,1)S(1)} collective-permute-done((bf16[2,64,1536]{2,1,0:T(8,128)(2,1)S(1)}, bf16[2,64,1536]{2,1,0:T(8,128)(2,1)S(1)}, u32[]{:S(2)}, u32[]{:S(2)}) %collective-permute-start.15) | collective-permute-done | bytes 393248 | tf_op jit(solution)/shard_map/ppermute | solution.py:297
  56.6 5.2 %load.7 = (s32[8,128]{1,0:T(8,128)}, bf16[1536,4096]{1,0:T(8,128)(2,1)S(1)}) custom-call(s32[1]{0:T(128)} %bitcast.refs_0_, bf16[2,64,1536]{2,1,0:T(8,128)(2,1)S(1)} %get-tuple-element.135.refs_1_, bf16[3584,4096]{1,0:T(8,128)(2,1)} %refs_7_.5), custom_call_target="tpu_custom_call" | custom-call | bytes 786432 | tf_op jit(solution)/shard_map/load/pallas_call | solution.py:74
  61.8 4.6 %down.3 = (f32[128,4096]{1,0:T(8,128)S(1)}, bf16[1536,4096]{1,0:T(8,128)(2,1)S(1)}) custom-call(s32[1]{0:T(128)} %bitcast.refs_0_, bf16[64,512]{1,0:T(8,128)(2,1)S(1)} %fusion.12.refs_1_, bf16[64,1536]{1,0:T(8,128)(2,1)S(1)} %fusion.5.refs_2_, bf16[64,512]{1,0:T(8,128)(2,1)S(1)} %collective-permute-done.16.refs_3_, ...), custom_call_target="tpu_custom_call" | custom-call | flops 134217728 | bytes 786432 | tf_op jit(solution)/shard_map/down/pallas_call | solution.py:74
  69.5 1.6 %collective-permute-start.20 = (bf16[64,2560]{1,0:T(8,128)(2,1)S(1)}, bf16[64,2560]{1,0:T(8,128)(2,1)S(1)}, u32[]{:S(2)}, u32[]{:S(2)}) collective-permute-start(bf16[64,2560]{1,0:T(8,128)(2,1)S(1)} %get-tuple-element.142.refs_5_), channel_id=1, source_target_pairs={{0,4},{4,0},{8,12},{12,8},{16,20},{20,16},{24,28},{28,24},{1,5},{5... | collective-permute-start | bytes 983048 | tf_op jit(solution)/shard_map/ppermute | solution.py:300
  72.7 2.9 %collective-permute-start.22 = (bf16[32,1536]{1,0:T(8,128)(2,1)S(1)}, bf16[32,1536]{1,0:T(8,128)(2,1)S(1)}, u32[]{:S(2)}, u32[]{:S(2)}) collective-permute-start(bf16[32,1536]{1,0:T(8,128)(2,1)S(1)} %get-tuple-element.144), channel_id=1, source_target_pairs={{0,16},{4,20},{8,24},{12,28},{16,0},{20,4},{24,8},{28,12},{1,17},{... | collective-permute-start | bytes 294920 | tf_op jit(solution)/shard_map/ppermute | solution.py:303
  76.4 3.1 %collective-permute-done.20 = bf16[64,2560]{1,0:T(8,128)(2,1)S(1)} collective-permute-done((bf16[64,2560]{1,0:T(8,128)(2,1)S(1)}, bf16[64,2560]{1,0:T(8,128)(2,1)S(1)}, u32[]{:S(2)}, u32[]{:S(2)}) %collective-permute-start.20) | collective-permute-done | bytes 327712 | tf_op jit(solution)/shard_map/ppermute | solution.py:300
  80.4 2.4 %collective-permute-start.26 = (bf16[16,2560]{1,0:T(8,128)(2,1)S(1)}, bf16[16,2560]{1,0:T(8,128)(2,1)S(1)}, u32[]{:S(2)}, u32[]{:S(2)}) collective-permute-start(bf16[16,2560]{1,0:T(8,128)(2,1)S(1)} %get-tuple-element.162), channel_id=1, source_target_pairs={{0,24},{4,28},{8,16},{12,20},{16,8},{20,12},{24,0},{28,4},{1,25},{... | collective-permute-start | bytes 245768 | tf_op jit(solution)/shard_map/ppermute | solution.py:303
  83.5 2.1 %collective-permute-done.24 = bf16[16,2560]{1,0:T(8,128)(2,1)S(1)} collective-permute-done((bf16[16,2560]{1,0:T(8,128)(2,1)S(1)}, bf16[16,2560]{1,0:T(8,128)(2,1)S(1)}, u32[]{:S(2)}, u32[]{:S(2)}) %collective-permute-start.24) | collective-permute-done | bytes 81952 | tf_op jit(solution)/shard_map/ppermute | solution.py:303
  86.2 1.3 %collective-permute-done.26 = bf16[16,2560]{1,0:T(8,128)(2,1)S(1)} collective-permute-done((bf16[16,2560]{1,0:T(8,128)(2,1)S(1)}, bf16[16,2560]{1,0:T(8,128)(2,1)S(1)}, u32[]{:S(2)}, u32[]{:S(2)}) %collective-permute-start.26) | collective-permute-done | bytes 81952 | tf_op jit(solution)/shard_map/ppermute | solution.py:303
  87.5 4.2 %collective-permute-done.25 = bf16[16,2560]{1,0:T(8,128)(2,1)S(1)} collective-permute-done((bf16[16,2560]{1,0:T(8,128)(2,1)S(1)}, bf16[16,2560]{1,0:T(8,128)(2,1)S(1)}, u32[]{:S(2)}, u32[]{:S(2)}) %collective-permute-start.25) | collective-permute-done | bytes 81952 | tf_op jit(solution)/shard_map/ppermute | solution.py:303
  95.6 1.8 %collective-permute-done.29 = bf16[4,4096]{1,0:T(4,128)(2,1)S(1)} collective-permute-done((bf16[4,4096]{1,0:T(4,128)(2,1)S(1)}, bf16[4,4096]{1,0:T(4,128)(2,1)S(1)}, u32[]{:S(2)}, u32[]{:S(2)}) %collective-permute-start.29) | collective-permute-done | bytes 32800 | tf_op jit(solution)/shard_map/ppermute | solution.py:297
  (76 shorter events, 21.1 us)
Async XLA Ops:
  3.5 6.6 %collective-permute-start.2 = (bf16[4,4096]{1,0:T(4,128)(2,1)S(1)}, bf16[4,4096]{1,0:T(4,128)(2,1)S(1)}, u32[]{:S(2)}, u32[]{:S(2)}) collective-permute-start(bf16[4,4096]{1,0:T(4,128)(2,1)S(1)} %get-tuple-element.174), channel_id=1, source_target_pairs={{0,3},{1,2},{2,1},{3,0},{4,7},{5,6},{6,5},{7,4},{8,11},{9,10},{10,... | collective-permute-start | bytes 98312 | tf_op jit(solution)/shard_map/ppermute | solution.py:297
  5.9 4.2 %collective-permute-start.1 = (bf16[4,4096]{1,0:T(4,128)(2,1)S(1)}, bf16[4,4096]{1,0:T(4,128)(2,1)S(1)}, u32[]{:S(2)}, u32[]{:S(2)}) collective-permute-start(bf16[4,4096]{1,0:T(4,128)(2,1)S(1)} %get-tuple-element.175), channel_id=1, source_target_pairs={{0,2},{1,3},{2,0},{3,1},{4,6},{5,7},{6,4},{7,5},{8,10},{9,11},{10,... | collective-permute-start | bytes 98312 | tf_op jit(solution)/shard_map/ppermute | solution.py:297
  10.3 6.3 %collective-permute-start.3 = (bf16[16,1536]{1,0:T(8,128)(2,1)S(1)}, bf16[16,1536]{1,0:T(8,128)(2,1)S(1)}, u32[]{:S(2)}, u32[]{:S(2)}) collective-permute-start(bf16[16,1536]{1,0:T(8,128)(2,1)S(1)} %pad_maximum_fusion.5), channel_id=1, source_target_pairs={{0,4},{4,0},{8,12},{12,8},{16,20},{20,16},{24,28},{28,24},{1,5},{5... | collective-permute-start | bytes 147464 | tf_op jit(solution)/shard_map/ppermute | solution.py:300
  12.1 10.4 %collective-permute-start.6 = (bf16[16,2560]{1,0:T(8,128)(2,1)S(1)}, bf16[16,2560]{1,0:T(8,128)(2,1)S(1)}, u32[]{:S(2)}, u32[]{:S(2)}) collective-permute-start(bf16[16,2560]{1,0:T(8,128)(2,1)S(1)} %pad_maximum_fusion.2.refs_5_), channel_id=1, source_target_pairs={{0,24},{4,28},{8,16},{12,20},{16,8},{20,12},{24,0},{28,4},{1,25},{... | collective-permute-start | bytes 245768 | tf_op jit(solution)/shard_map/ppermute | solution.py:303
  15.8 7.0 %collective-permute-start.5 = (bf16[16,2560]{1,0:T(8,128)(2,1)S(1)}, bf16[16,2560]{1,0:T(8,128)(2,1)S(1)}, u32[]{:S(2)}, u32[]{:S(2)}) collective-permute-start(bf16[16,2560]{1,0:T(8,128)(2,1)S(1)} %pad_maximum_fusion.2.refs_5_), channel_id=1, source_target_pairs={{0,16},{4,20},{8,24},{12,28},{16,0},{20,4},{24,8},{28,12},{1,17},{... | collective-permute-start | bytes 245768 | tf_op jit(solution)/shard_map/ppermute | solution.py:303
  15.8 7.0 %collective-permute-start.4 = (bf16[16,2560]{1,0:T(8,128)(2,1)S(1)}, bf16[16,2560]{1,0:T(8,128)(2,1)S(1)}, u32[]{:S(2)}, u32[]{:S(2)}) collective-permute-start(bf16[16,2560]{1,0:T(8,128)(2,1)S(1)} %pad_maximum_fusion.2.refs_5_), channel_id=1, source_target_pairs={{0,8},{4,12},{8,0},{12,4},{16,24},{20,28},{24,16},{28,20},{1,9},{5... | collective-permute-start | bytes 245768 | tf_op jit(solution)/shard_map/ppermute | solution.py:303
  22.8 11.4 %collective-permute-start.10 = (bf16[64,2560]{1,0:T(8,128)(2,1)S(1)}, bf16[64,2560]{1,0:T(8,128)(2,1)S(1)}, u32[]{:S(2)}, u32[]{:S(2)}) collective-permute-start(bf16[64,2560]{1,0:T(8,128)(2,1)S(1)} %pad_maximum_fusion), channel_id=1, source_target_pairs={{0,4},{4,0},{8,12},{12,8},{16,20},{20,16},{24,28},{28,24},{1,5},{5... | collective-permute-start | bytes 983048 | tf_op jit(solution)/shard_map/ppermute | solution.py:300
  23.4 10.3 %collective-permute-start.9 = (bf16[32,1536]{1,0:T(8,128)(2,1)S(1)}, bf16[32,1536]{1,0:T(8,128)(2,1)S(1)}, u32[]{:S(2)}, u32[]{:S(2)}) collective-permute-start(bf16[32,1536]{1,0:T(8,128)(2,1)S(1)} %pad_maximum_fusion.1.refs_1_), channel_id=1, source_target_pairs={{0,24},{4,28},{8,16},{12,20},{16,8},{20,12},{24,0},{28,4},{1,25},{... | collective-permute-start | bytes 294920 | tf_op jit(solution)/shard_map/ppermute | solution.py:303
  26.8 7.3 %collective-permute-start.8 = (bf16[32,1536]{1,0:T(8,128)(2,1)S(1)}, bf16[32,1536]{1,0:T(8,128)(2,1)S(1)}, u32[]{:S(2)}, u32[]{:S(2)}) collective-permute-start(bf16[32,1536]{1,0:T(8,128)(2,1)S(1)} %pad_maximum_fusion.1.refs_1_), channel_id=1, source_target_pairs={{0,16},{4,20},{8,24},{12,28},{16,0},{20,4},{24,8},{28,12},{1,17},{... | collective-permute-start | bytes 294920 | tf_op jit(solution)/shard_map/ppermute | solution.py:303
  26.8 7.3 %collective-permute-start.7 = (bf16[32,1536]{1,0:T(8,128)(2,1)S(1)}, bf16[32,1536]{1,0:T(8,128)(2,1)S(1)}, u32[]{:S(2)}, u32[]{:S(2)}) collective-permute-start(bf16[32,1536]{1,0:T(8,128)(2,1)S(1)} %pad_maximum_fusion.1.refs_1_), channel_id=1, source_target_pairs={{0,8},{4,12},{8,0},{12,4},{16,24},{20,28},{24,16},{28,20},{1,9},{5... | collective-permute-start | bytes 294920 | tf_op jit(solution)/shard_map/ppermute | solution.py:303
  37.0 5.6 %collective-permute-start.13 = (bf16[2,64,512]{2,1,0:T(8,128)(2,1)S(1)}, bf16[2,64,512]{2,1,0:T(8,128)(2,1)S(1)}, u32[]{:S(2)}, u32[]{:S(2)}) collective-permute-start(bf16[2,64,512]{2,1,0:T(8,128)(2,1)S(1)} %fusion.7.refs_8_), channel_id=1, source_target_pairs={{0,2},{1,3},{2,0},{3,1},{4,6},{5,7},{6,4},{7,5},{8,10},{9,11},{10,... | collective-permute-start | bytes 393224 | tf_op jit(solution)/shard_map/ppermute | solution.py:297
  43.9 11.2 %collective-permute-start.15 = (bf16[2,64,1536]{2,1,0:T(8,128)(2,1)S(1)}, bf16[2,64,1536]{2,1,0:T(8,128)(2,1)S(1)}, u32[]{:S(2)}, u32[]{:S(2)}) collective-permute-start(bf16[2,64,1536]{2,1,0:T(8,128)(2,1)S(1)} %fusion.refs_4_), channel_id=1, source_target_pairs={{0,2},{1,3},{2,0},{3,1},{4,6},{5,7},{6,4},{7,5},{8,10},{9,11},{10,... | collective-permute-start | bytes 1179656 | tf_op jit(solution)/shard_map/ppermute | solution.py:297
  44.5 11.0 %collective-permute-start.16 = (bf16[64,512]{1,0:T(8,128)(2,1)S(1)}, bf16[64,512]{1,0:T(8,128)(2,1)S(1)}, u32[]{:S(2)}, u32[]{:S(2)}) collective-permute-start(bf16[64,512]{1,0:T(8,128)(2,1)S(1)} %fusion.12.refs_1_), channel_id=1, source_target_pairs={{0,1},{1,0},{2,3},{3,2},{4,5},{5,4},{6,7},{7,6},{8,9},{9,8},{10,11... | collective-permute-start | bytes 196616 | tf_op jit(solution)/shard_map/ppermute | solution.py:297
  55.5 10.9 %collective-permute-start.18 = (bf16[2,64,1536]{2,1,0:T(8,128)(2,1)S(1)}, bf16[2,64,1536]{2,1,0:T(8,128)(2,1)S(1)}, u32[]{:S(2)}, u32[]{:S(2)}) collective-permute-start(bf16[2,64,1536]{2,1,0:T(8,128)(2,1)S(1)} %get-tuple-element.135.refs_1_), channel_id=1, source_target_pairs={{0,2},{1,3},{2,0},{3,1},{4,6},{5,7},{6,4},{7,5},{8,10},{9,11},{10,... | collective-permute-start | bytes 1179656 | tf_op jit(solution)/shard_map/ppermute | solution.py:297
  56.6 5.3 %collective-permute-start.17 = (bf16[64,1536]{1,0:T(8,128)(2,1)S(1)}, bf16[64,1536]{1,0:T(8,128)(2,1)S(1)}, u32[]{:S(2)}, u32[]{:S(2)}) collective-permute-start(bf16[64,1536]{1,0:T(8,128)(2,1)S(1)} %fusion.5.refs_2_), channel_id=1, source_target_pairs={{0,1},{1,0},{2,3},{3,2},{4,5},{5,4},{6,7},{7,6},{8,9},{9,8},{10,11... | collective-permute-start | bytes 589832 | tf_op jit(solution)/shard_map/ppermute | solution.py:297
  69.5 10.1 %collective-permute-start.20 = (bf16[64,2560]{1,0:T(8,128)(2,1)S(1)}, bf16[64,2560]{1,0:T(8,128)(2,1)S(1)}, u32[]{:S(2)}, u32[]{:S(2)}) collective-permute-start(bf16[64,2560]{1,0:T(8,128)(2,1)S(1)} %get-tuple-element.142.refs_5_), channel_id=1, source_target_pairs={{0,4},{4,0},{8,12},{12,8},{16,20},{20,16},{24,28},{28,24},{1,5},{5... | collective-permute-start | bytes 983048 | tf_op jit(solution)/shard_map/ppermute | solution.py:300
  72.0 10.8 %collective-permute-start.21 = (bf16[32,1536]{1,0:T(8,128)(2,1)S(1)}, bf16[32,1536]{1,0:T(8,128)(2,1)S(1)}, u32[]{:S(2)}, u32[]{:S(2)}) collective-permute-start(bf16[32,1536]{1,0:T(8,128)(2,1)S(1)} %get-tuple-element.143), channel_id=1, source_target_pairs={{0,8},{4,12},{8,0},{12,4},{16,24},{20,28},{24,16},{28,20},{1,9},{5... | collective-permute-start | bytes 294920 | tf_op jit(solution)/shard_map/ppermute | solution.py:303
  72.7 10.8 %collective-permute-start.22 = (bf16[32,1536]{1,0:T(8,128)(2,1)S(1)}, bf16[32,1536]{1,0:T(8,128)(2,1)S(1)}, u32[]{:S(2)}, u32[]{:S(2)}) collective-permute-start(bf16[32,1536]{1,0:T(8,128)(2,1)S(1)} %get-tuple-element.144), channel_id=1, source_target_pairs={{0,16},{4,20},{8,24},{12,28},{16,0},{20,4},{24,8},{28,12},{1,17},{... | collective-permute-start | bytes 294920 | tf_op jit(solution)/shard_map/ppermute | solution.py:303
  75.6 7.9 %collective-permute-start.23 = (bf16[32,1536]{1,0:T(8,128)(2,1)S(1)}, bf16[32,1536]{1,0:T(8,128)(2,1)S(1)}, u32[]{:S(2)}, u32[]{:S(2)}) collective-permute-start(bf16[32,1536]{1,0:T(8,128)(2,1)S(1)} %get-tuple-element.145), channel_id=1, source_target_pairs={{0,24},{4,28},{8,16},{12,20},{16,8},{20,12},{24,0},{28,4},{1,25},{... | collective-permute-start | bytes 294920 | tf_op jit(solution)/shard_map/ppermute | solution.py:303
  79.7 5.9 %collective-permute-start.24 = (bf16[16,2560]{1,0:T(8,128)(2,1)S(1)}, bf16[16,2560]{1,0:T(8,128)(2,1)S(1)}, u32[]{:S(2)}, u32[]{:S(2)}) collective-permute-start(bf16[16,2560]{1,0:T(8,128)(2,1)S(1)} %get-tuple-element.161), channel_id=1, source_target_pairs={{0,8},{4,12},{8,0},{12,4},{16,24},{20,28},{24,16},{28,20},{1,9},{5... | collective-permute-start | bytes 245768 | tf_op jit(solution)/shard_map/ppermute | solution.py:303
  80.4 7.2 %collective-permute-start.26 = (bf16[16,2560]{1,0:T(8,128)(2,1)S(1)}, bf16[16,2560]{1,0:T(8,128)(2,1)S(1)}, u32[]{:S(2)}, u32[]{:S(2)}) collective-permute-start(bf16[16,2560]{1,0:T(8,128)(2,1)S(1)} %get-tuple-element.162), channel_id=1, source_target_pairs={{0,24},{4,28},{8,16},{12,20},{16,8},{20,12},{24,0},{28,4},{1,25},{... | collective-permute-start | bytes 245768 | tf_op jit(solution)/shard_map/ppermute | solution.py:303
  82.8 8.9 %collective-permute-start.25 = (bf16[16,2560]{1,0:T(8,128)(2,1)S(1)}, bf16[16,2560]{1,0:T(8,128)(2,1)S(1)}, u32[]{:S(2)}, u32[]{:S(2)}) collective-permute-start(bf16[16,2560]{1,0:T(8,128)(2,1)S(1)} %get-tuple-element.163), channel_id=1, source_target_pairs={{0,16},{4,20},{8,24},{12,28},{16,0},{20,4},{24,8},{28,12},{1,17},{... | collective-permute-start | bytes 245768 | tf_op jit(solution)/shard_map/ppermute | solution.py:303
  85.6 6.2 %collective-permute-start.27 = (bf16[16,1536]{1,0:T(8,128)(2,1)S(1)}, bf16[16,1536]{1,0:T(8,128)(2,1)S(1)}, u32[]{:S(2)}, u32[]{:S(2)}) collective-permute-start(bf16[16,1536]{1,0:T(8,128)(2,1)S(1)} %slice.123), channel_id=1, source_target_pairs={{0,4},{4,0},{8,12},{12,8},{16,20},{20,16},{24,28},{28,24},{1,5},{5... | collective-permute-start | bytes 147464 | tf_op jit(solution)/shard_map/ppermute | solution.py:300
  93.5 3.9 %collective-permute-start.29 = (bf16[4,4096]{1,0:T(4,128)(2,1)S(1)}, bf16[4,4096]{1,0:T(4,128)(2,1)S(1)}, u32[]{:S(2)}, u32[]{:S(2)}) collective-permute-start(bf16[4,4096]{1,0:T(4,128)(2,1)S(1)} %get-tuple-element.169), channel_id=1, source_target_pairs={{0,2},{1,3},{2,0},{3,1},{4,6},{5,7},{6,4},{7,5},{8,10},{9,11},{10,... | collective-permute-start | bytes 98312 | tf_op jit(solution)/shard_map/ppermute | solution.py:297
  (7 other events, 16.5 us)
